TPU v7x, 32 devices: a whole 2x2x4 slice. The times are simulated.
32 devices in a mesh: dp: 4 (over x, core), ctx: 2 (over y), tp: 4 (over z).
Axes of the slice: x: 2, y: 2, z: 4, core: 2. Of those that a mesh axis runs over, the one named last changes fastest.
Arguments:
- upstream: bfloat16 [1024, 3072], P(('dp', 'ctx'), 'tp'), may hold values from -6 to 6
- router_logits: float32 [1024, 2], P(('dp', 'ctx')), may hold values from -6 to 6
- expert_ids: int32 [1024, 2], P(('dp', 'ctx')), may hold values from 0 to 7, all different within a row; in each aligned block of 128 rows (0 to 127, 128 to 255, ...) at most 36 rows name the same one
- hidden_saved: bfloat16 [288, 65536], P('dp', ('ctx', 'tp')), may hold values from -0.75 to 0.75
- down_weight: bfloat16 [65536, 3072], P(('ctx', 'tp'), 'dp'), may hold values from -0.0625 to 0.0625
Outputs:
- hidden_grad: bfloat16 [288, 65536], P('dp', ('ctx', 'tp'))
- down_grad: bfloat16 [65536, 3072], P(('ctx', 'tp'), 'dp')
- logit_grad: float32 [1024, 2], P(('dp', 'ctx'))
Inputs may be any that keep to these rules, and one draw needn't show every extreme that they name: `expert_ids`: the ids of a row differ; in each aligned block of 128 rows (the rows of one device) no expert is named more than 36 times.
All inputs are finite; a program needn't handle non-finite values.
Results may differ from a plain program's by a relative error of at most 0.013.
Values may be sent and summed in bfloat16 or wider, within the bound.
A program may use at most 192 MiB of HBM per device.

v0:
```python
import jax
import jax.numpy as jnp
from jax import lax
from jax.sharding import PartitionSpec as P

EXPERTS = 8
TOP = 2


def pack_rows(columns, token_place):
    packed = lax.dot_general(
        token_place, columns, (((0,), (0,)), ((), ())), preferred_element_type=jnp.float32
    )
    return packed.astype(jnp.bfloat16)


def local(upstream, router_logits, expert_ids, hidden_saved, down_weight):
    token_count = upstream.shape[0]
    tensor_count = lax.axis_size("tp")
    context_count = lax.axis_size("ctx")
    block_count = context_count * tensor_count
    capacity = hidden_saved.shape[0] // context_count
    gates = 1.0 / (1.0 + jnp.exp(router_logits[:, ::-1] - router_logits))
    gates_sent = gates.astype(jnp.bfloat16)
    routes = expert_ids.reshape(-1)
    onehot = (routes[:, None] == jnp.arange(EXPERTS, dtype=jnp.int32)[None, :]).astype(jnp.int32)
    earlier = jnp.cumsum(onehot, axis=0) - onehot
    slot = jnp.sum(earlier * onehot, axis=1)
    position = routes * capacity + slot
    place = (position[:, None] == jnp.arange(EXPERTS * capacity, dtype=jnp.int32)[None, :]).astype(
        jnp.float32
    )
    token_place = (
        place.reshape(token_count, TOP, EXPERTS * capacity).sum(axis=1).astype(jnp.bfloat16)
    )
    gate_packed = jnp.sum(
        place * gates_sent.reshape(-1).astype(jnp.float32)[:, None], axis=0
    ).astype(jnp.bfloat16)
    group_size = block_count // EXPERTS
    packed = pack_rows(upstream, token_place)
    feature_cols = packed.shape[1]
    outgoing = jnp.broadcast_to(
        packed.reshape(EXPERTS, 1, capacity, feature_cols),
        (EXPERTS, group_size, capacity, feature_cols),
    ).reshape(block_count, capacity, feature_cols)
    gate_out = jnp.broadcast_to(
        gate_packed.reshape(EXPERTS, 1, capacity), (EXPERTS, group_size, capacity)
    ).reshape(block_count, capacity)
    received, gate_in = (
        lax.all_to_all(outgoing, ("ctx", "tp"), split_axis=0, concat_axis=0, tiled=True),
        lax.all_to_all(gate_out, ("ctx", "tp"), split_axis=0, concat_axis=0, tiled=True),
    )
    rows = received.reshape(context_count, tensor_count, capacity, feature_cols)
    rows = rows.transpose(0, 2, 1, 3).reshape(context_count * capacity, tensor_count * feature_cols)
    gate_rows = gate_in.reshape(context_count, tensor_count, capacity)[:, 0, :].reshape(-1)
    proj = lax.dot_general(
        rows,
        lax.all_gather(down_weight, "dp", axis=1, tiled=True),
        (((1,), (1,)), ((), ())),
        preferred_element_type=jnp.float32,
    )
    gate_column = gate_rows.astype(jnp.float32)[:, None]
    hidden_grad = (gate_column * proj).astype(jnp.bfloat16)
    weighted = (gate_column * rows.astype(jnp.float32)).astype(jnp.bfloat16)
    product = lax.dot_general(
        hidden_saved, weighted, (((0,), (0,)), ((), ())), preferred_element_type=jnp.float32
    )
    down_grad = lax.psum_scatter(
        product.astype(jnp.bfloat16), "dp", scatter_dimension=1, tiled=True
    )
    partial_value = jnp.sum(hidden_saved.astype(jnp.float32) * proj, axis=1).reshape(
        context_count, capacity
    )
    group_size = block_count // EXPERTS
    outgoing_parts = jnp.broadcast_to(
        partial_value[:, None, :], (context_count, tensor_count, capacity)
    ).reshape(block_count, capacity)
    returned = lax.all_to_all(
        outgoing_parts, ("ctx", "tp"), split_axis=0, concat_axis=0, tiled=True
    )
    expert_sums = returned.reshape(EXPERTS, group_size, capacity).sum(axis=1)
    route_grad = jnp.take(expert_sums.reshape(-1), position).reshape(token_count, TOP)
    logit_grad = gates * (route_grad - jnp.sum(gates * route_grad, axis=1, keepdims=True))
    return (hidden_grad, down_grad, logit_grad)


def solution(mesh):
    in_specs = (
        P(("dp", "ctx"), "tp"),
        P(("dp", "ctx"), None),
        P(("dp", "ctx"), None),
        P("dp", ("ctx", "tp")),
        P(("ctx", "tp"), "dp"),
    )
    out_specs = (P("dp", ("ctx", "tp")), P(("ctx", "tp"), "dp"), P(("dp", "ctx"), None))
    return jax.shard_map(local, mesh=mesh, in_specs=in_specs, out_specs=out_specs, check_vma=False)
```

profile of v0, /device:TPU:0, one launch (start us, length us, event | category | flops | bytes accessed | tf_op | source)
XLA Modules:
  0.0 681.2 jit_solution(1859538189464288882)
XLA Ops:
  7.2 0.7 all-gather.2.cloned.1.call-update
  7.9 0.1 copy.27
  8.1 0.1 reshape.132
  8.2 0.1 eq.46
  8.6 0.6 reduce-window.6
  9.1 0.2 slice_reduce_fusion
  9.4 0.1 reshape.138
  9.7 0.1 select_reduce_fusion
  9.8 0.7 convert_element_type.92
  10.5 7.3 %all-to-all-start = ((bf16[8,1,36]{2,1,0:T(2,128)(2,1)}), bf16[8,1,36]{2,1,0:T(2,128)(2,1)S(1)}, u32[]{:S(2)}, u32[]{:S(2)}) async-start(bf16[8,1,36]{2,1,0:T(2,128)(2,1)} %convert_element_type.92), calls=%async_computation | async-start | bytes 8192 | tf_op jit(solution)/shard_map/all_to_all | solution.py:51
  17.8 0.1 reduce_sum.55
  18.1 0.3 convolution_convert_fusion
  18.4 0.9 reshape_reshape.4
  19.2 5.0 all-to-all-done
  24.2 3.5 all-to-all-start.1
  27.9 13.3 %all-to-all-done.1 = bf16[8,36,768]{2,1,0:T(8,128)(2,1)S(1)} async-done(((bf16[8,36,768]{2,1,0:T(8,128)(2,1)}), bf16[8,36,768]{2,1,0:T(8,128)(2,1)S(1)}, u32[]{:S(2)}, u32[]{:S(2)}) %all-to-all-start.1) | async-done | bytes 442400 | tf_op jit(solution)/shard_map/all_to_all | solution.py:50
  41.2 0.2 copy.34
  41.4 21.4 %convert_bitcast_fusion = bf16[8192,3072]{0,1:T(8,128)(2,1)} fusion(bf16[72,8192]{1,0:T(8,128)(2,1)S(1)} %copy-done.2, bf16[72,3072]{1,0:T(8,128)(2,1)S(1)} %bitcast.26, f32[72]{0:T(128)S(1)} %reshape.139), kind=kOutput, calls=%fused_computation.1 | convolution fusion | flops 3649708032 | bytes 51953952 | tf_op jit(solution)/shard_map/dot_general | solution.py:65
  62.9 0.1 mul.75
  63.1 248.9 %all-gather.2.cloned.1.call-done = bf16[8192,3072]{1,0:T(8,128)(2,1)} async-done(((bf16[8192,768]{1,0:T(8,128)(2,1)}), bf16[8192,3072]{1,0:T(8,128)(2,1)}) %all-gather.2.cloned.1.call-update) | async-done | bytes 50331664 | tf_op jit(solution)/shard_map/all_gather | solution.py:58
  311.9 27.6 %multiply_reduce_fusion = (f32[72]{0:T(128)S(1)}, bf16[72,8192]{1,0:T(8,128)(2,1)}) fusion(bf16[72,8192]{1,0:T(8,128)(2,1)S(1)} %copy-done.2, f32[72]{0:T(128)S(1)} %reshape.139, bf16[72,3072]{1,0:T(8,128)(2,1)S(1)} %bitcast.27, bf16[8192,3072]{1,0:T(8,128)(2,1)} %all-gather.2.cloned.1.call-done), kind=kOutput, calls=%fused_computation.2 | convolution fusion | flops 3626827776 | bytes 53133888 | tf_op jit(solution)/shard_map/dot_general | solution.py:56
  339.6 0.6 broadcast_in_dim.9
  340.2 5.4 all-to-all-start.2
  345.6 6.4 all-to-all-done.2
  352.0 0.5 broadcast.96
  352.5 0.7 reduce.9
  353.3 1.9 gather_fusion
  355.2 0.1 gather.7
  355.4 0.1 multiply_reduce_fusion.1
  355.6 0.6 copy.36
  356.2 301.6 %reduce-scatter.2.cloned.1.call-done = bf16[8192,768]{0,1:T(8,128)(2,1)} async-done(((bf16[8192,3072]{0,1:T(8,128)(2,1)}), bf16[8192,768]{0,1:T(8,128)(2,1)}) %reduce-scatter.2.cloned.1.call-update) | async-done | bytes 12582928 | tf_op jit(solution)/shard_map/reduce_scatter | solution.py:68
  657.8 16.6 %copy.35 = bf16[8192,768]{1,0:T(8,128)(2,1)} copy(bf16[8192,768]{0,1:T(8,128)(2,1)} %reduce-scatter.2.cloned.1.call-done) | data formatting | bytes 25165824
  (33 shorter events, 1.0 us)
Async XLA Ops:
  7.2 10.9 %copy-start = (bf16[128,768]{1,0:T(8,128)(2,1)S(1)}, bf16[128,768]{1,0:T(8,128)(2,1)}, u32[]{:S(2)}) copy-start(bf16[128,768]{1,0:T(8,128)(2,1)} %param.5) | copy-start | bytes 589828
  7.2 0.8 copy-start.3
  7.2 1.2 copy-start.4
  7.2 304.7 %all-gather.2.cloned.1.call-start = ((), (), s32[]{:S(2)}) async-start(), calls=%async_computation.4 | async-start | bytes 62914560 | tf_op jit(solution)/shard_map/all_gather | solution.py:58
  10.5 13.7 %all-to-all-start = ((bf16[8,1,36]{2,1,0:T(2,128)(2,1)}), bf16[8,1,36]{2,1,0:T(2,128)(2,1)S(1)}, u32[]{:S(2)}, u32[]{:S(2)}) async-start(bf16[8,1,36]{2,1,0:T(2,128)(2,1)} %convert_element_type.92), calls=%async_computation | async-start | bytes 8192 | tf_op jit(solution)/shard_map/all_to_all | solution.py:51
  18.0 23.5 %copy-start.2 = (bf16[72,8192]{1,0:T(8,128)(2,1)S(1)}, bf16[72,8192]{1,0:T(8,128)(2,1)}, u32[]{:S(2)}) copy-start(bf16[72,8192]{1,0:T(8,128)(2,1)} %param.8) | copy-start | bytes 3538948
  24.2 17.0 %all-to-all-start.1 = ((bf16[8,36,768]{2,1,0:T(8,128)(2,1)}), bf16[8,36,768]{2,1,0:T(8,128)(2,1)S(1)}, u32[]{:S(2)}, u32[]{:S(2)}) async-start(bf16[8,36,768]{2,1,0:T(8,128)(2,1)} %reshape_reshape.4), calls=%async_computation.1 | async-start | bytes 983040 | tf_op jit(solution)/shard_map/all_to_all | solution.py:50
  27.7 630.1 %reduce-scatter.2.cloned.1.call-start = ((), (), s32[]{:S(2)}) async-start(), calls=%async_computation.5 | async-start | bytes 62914560 | tf_op jit(solution)/shard_map/reduce_scatter | solution.py:68
  340.2 11.8 %all-to-all-start.2 = ((f32[8,1,36]{2,1,0:T(1,128)}), f32[8,1,36]{2,1,0:T(1,128)S(1)}, u32[]{:S(2)}, u32[]{:S(2)}) async-start(f32[8,1,36]{2,1,0:T(1,128)} %bitcast.5), calls=%async_computation.3 | async-start | bytes 8192 | tf_op jit(solution)/shard_map/all_to_all | solution.py:78
  657.8 16.6 %copy-start.1 = (bf16[128,768]{1,0:T(8,128)(2,1)S(1)}, bf16[128,768]{1,0:T(8,128)(2,1)}, u32[]{:S(2)}) copy-start(bf16[128,768]{1,0:T(8,128)(2,1)} %param.5) | copy-start | bytes 589828
Sparse Core Ops, SparseCore 0:
  9.6 302.2 all-gather.1
  314.5 343.1 reduce-scatter.1
where the time goes:
time: 682 us; the launch traced here: 681 us
  waiting for transfers between devices  576 us (84%)
  matrix products  49.3 us (7%)
  local copies, waits for them, and re-layouts  23.8 us (3%)
  starting transfers between devices  16.2 us (2%)
  between operations  14.2 us (2%)
    reduce_scatter x1, waiting for transfers between devices, local(): lax.psum_scatter(product.astype(jnp.bfloat16), 'dp', scatter_dimension=1,...  302 us
    all_gather x1, waiting for transfers between devices, local(): lax.all_gather(down_weight, 'dp', axis=1, tiled=True)  249 us
    dot_general x1, matrix products, local(): lax.dot_general(rows, lax.all_gather(down_weight, 'dp', axis=1, tiled=Tru...  27.6 us
    dot_general x1, matrix products, local(): lax.dot_general(hidden_saved, weighted, (((0,), (0,)), ((), ())), preferr...  21.4 us
    unnamed x16, local copies, waits for them, and re-layouts  17.6 us
  transfers between devices with their start and end apart: 5, of which 5 were waited for; matrix products, arithmetic and copies ran while one was open for 9% of the time, Pallas kernels for 0%

commit v1 on v0

v1 whole, which is shorter than its diff:
```python
import jax
import jax.numpy as jnp
from jax import lax
from jax.sharding import PartitionSpec as P

EXPERTS = 8
TOP = 2


def swap(value, distance):
    count = lax.axis_size("dp")
    return lax.ppermute(value, "dp", [(i, i ^ distance) for i in range(count)])


def local(upstream, router_logits, expert_ids, hidden_saved, down_weight):
    token_count, feature_cols = upstream.shape
    dp_count = lax.axis_size("dp")
    tensor_count = lax.axis_size("tp")
    context_count = lax.axis_size("ctx")
    block_count = context_count * tensor_count
    slots = hidden_saved.shape[0]
    capacity = slots // context_count
    group_size = block_count // EXPERTS
    own_cols = down_weight.shape[1]
    me = lax.axis_index("dp")

    saved_cross = swap(hidden_saved, 2)
    saved_near = swap(hidden_saved, 1)

    gates = 1.0 / (1.0 + jnp.exp(router_logits[:, ::-1] - router_logits))
    gates_sent = gates.astype(jnp.bfloat16)
    routes = expert_ids.reshape(-1)
    onehot = routes[:, None] == jnp.arange(EXPERTS, dtype=jnp.int32)[None, :]
    number = jnp.arange(token_count * TOP, dtype=jnp.int32)
    earlier = lax.dot_general(
        (number[:, None] > number[None, :]).astype(jnp.bfloat16),
        onehot.astype(jnp.bfloat16),
        (((1,), (0,)), ((), ())),
        preferred_element_type=jnp.float32,
    )
    slot = jnp.sum(jnp.where(onehot, earlier, 0.0), axis=1).astype(jnp.int32)
    position = routes * capacity + slot
    place = (position[:, None] == jnp.arange(EXPERTS * capacity, dtype=jnp.int32)[None, :]).astype(
        jnp.float32
    )
    token_place = (
        place.reshape(token_count, TOP, EXPERTS * capacity).sum(axis=1).astype(jnp.bfloat16)
    )
    gate_packed = jnp.sum(
        place * gates_sent.reshape(-1).astype(jnp.float32)[:, None], axis=0
    ).astype(jnp.bfloat16)
    packed = lax.dot_general(
        token_place, upstream, (((0,), (0,)), ((), ())), preferred_element_type=jnp.float32
    ).astype(jnp.bfloat16)

    def spread(value):
        width = value.shape[-1]
        return jnp.broadcast_to(
            value.reshape(EXPERTS, 1, capacity, width), (EXPERTS, group_size, capacity, width)
        ).reshape(block_count, capacity, width)

    received = lax.all_to_all(spread(packed), ("ctx", "tp"), split_axis=0, concat_axis=0, tiled=True)
    gate_in = lax.all_to_all(
        spread(gate_packed[:, None]), ("ctx", "tp"), split_axis=0, concat_axis=0, tiled=True
    )
    rows = received.reshape(context_count, tensor_count, capacity, feature_cols)
    rows = rows.transpose(0, 2, 1, 3).reshape(slots, tensor_count * feature_cols)
    gate_own = gate_in.reshape(context_count, tensor_count, capacity)[:, 0, :].reshape(slots)
    rows = rows.reshape(slots, dp_count, own_cols).transpose(1, 0, 2)
    rows = lax.all_to_all(rows, "dp", split_axis=0, concat_axis=0, tiled=True)
    gate_all = lax.all_gather(gate_own, "dp")

    def ordered(value):
        return [lax.dynamic_index_in_dim(value, me ^ m, 0, keepdims=False) for m in range(4)]

    rows = ordered(rows)
    gate_rows = jnp.concatenate(ordered(gate_all)).astype(jnp.float32)[:, None]

    def project(value):
        return lax.dot_general(
            value, down_weight, (((1,), (1,)), ((), ())), preferred_element_type=jnp.float32
        )

    far = project(jnp.concatenate(rows[2:])).astype(jnp.bfloat16)
    far_near = swap(far[slots:], 1)
    far_sum = (far[:slots].astype(jnp.float32) + far_near.astype(jnp.float32)).astype(jnp.bfloat16)
    cross = swap(far_sum, 2)

    near = project(jnp.concatenate(rows[:2])).astype(jnp.bfloat16)
    near_in = swap(near[slots:], 1)

    saved_far = swap(saved_cross, 1)
    saved = jnp.concatenate([hidden_saved, saved_near, saved_cross, saved_far])
    weighted = (gate_rows * jnp.concatenate(rows).astype(jnp.float32)).astype(jnp.bfloat16)
    down_grad = lax.dot_general(
        saved, weighted, (((0,), (0,)), ((), ())), preferred_element_type=jnp.float32
    ).astype(jnp.bfloat16)

    def parts(left, right):
        return jnp.sum(left.astype(jnp.float32) * right.astype(jnp.float32), axis=1)

    part = jnp.stack(
        [
            parts(hidden_saved, near[:slots]),
            parts(saved_near, near[slots:]),
            parts(saved_cross, far[:slots]),
            parts(saved_far, far[slots:]),
        ]
    )
    part = jnp.stack([lax.dynamic_index_in_dim(part, me ^ m, 0, keepdims=False) for m in range(4)])
    every = lax.all_gather(part, ("dp", "ctx", "tp"))
    every = every.reshape(dp_count, EXPERTS, group_size, dp_count, context_count, capacity)
    mine = lax.dynamic_index_in_dim(every, me, 3, keepdims=False)
    mine = lax.dynamic_index_in_dim(mine, lax.axis_index("ctx"), 3, keepdims=False)
    expert_sums = mine.sum(axis=(0, 2)).reshape(-1)
    route_grad = jnp.sum(place * expert_sums[None, :], axis=1).reshape(token_count, TOP)
    logit_grad = gates * (route_grad - jnp.sum(gates * route_grad, axis=1, keepdims=True))

    proj = (
        near[:slots].astype(jnp.float32) + near_in.astype(jnp.float32) + cross.astype(jnp.float32)
    )
    hidden_grad = (gate_own.astype(jnp.float32)[:, None] * proj).astype(jnp.bfloat16)
    return (hidden_grad, down_grad, logit_grad)


def solution(mesh):
    in_specs = (
        P(("dp", "ctx"), "tp"),
        P(("dp", "ctx"), None),
        P(("dp", "ctx"), None),
        P("dp", ("ctx", "tp")),
        P(("ctx", "tp"), "dp"),
    )
    out_specs = (P("dp", ("ctx", "tp")), P(("ctx", "tp"), "dp"), P(("dp", "ctx"), None))
    return jax.shard_map(local, mesh=mesh, in_specs=in_specs, out_specs=out_specs, check_vma=False)
```

time: 682 us -> 191 us (0.28)
  waiting for transfers between devices: 576 us -> 24 us
  blocking collectives: 0 us -> 107 us
  matrix products: 49.3 us -> 29.5 us
  local copies, waits for them, and re-layouts: 23.8 us -> 8.06 us
  between operations: 14.2 us -> 0.86 us
  other arithmetic: 1.89 us -> 10.9 us
    reduce_scatter x1 -> x0, waiting for transfers between devices: 302 us -> none  [local(): lax.psum_scatter(product.astype(jnp.bfloat16), 'dp', scatter_dimension=1,...]
    all_gather x1 -> x0, waiting for transfers between devices: 249 us -> none  [local(): lax.all_gather(down_weight, 'dp', axis=1, tiled=True)]
    all_gather x0 -> x2, blocking collectives: none -> 84.8 us  [the longest x1 63.8 us: local(): every = lax.all_gather(part, ('dp', 'ctx', 'tp'))]
    all_to_all x0 -> x1, blocking collectives: none -> 21.8 us  [local(): lax.all_to_all(spread(packed), ('ctx', 'tp'), split_axis=0, concat_axis=0...]
    dot_general x3 -> x5, matrix products: 49.3 us -> 29.5 us  [the longest x2 17.6 us: project(): lax.dot_general(value, down_weight, (((1,), (1,)), ((), ())), preferred_e...]
    unnamed x16 -> x13, local copies, waits for them, and re-layouts: 17.6 us -> 3.08 us
    all_to_all x3 -> x2, waiting for transfers between devices: 24.6 us -> 10.4 us  [the longest x1 6.18 us: local(): rows = lax.all_to_all(rows, 'dp', split_axis=0, concat_axis=0, tiled=True)]
    ppermute x0 -> x6, waiting for transfers between devices: none -> 13.6 us  [swap(): return lax.ppermute(value, 'dp', [(i, i ^ distance) for i in range(count)])]
  transfers between devices with their start and end apart: 5 -> 8, of which waited for: 5 -> 3; matrix products, arithmetic and copies ran while one was open for 9% -> 21% of each run, Pallas kernels for 0% -> 0%
where the time goes in v1:
time: 191 us
  blocking collectives  107 us (56%)
  matrix products  29.5 us (15%)
  waiting for transfers between devices  24 us (13%)
  other arithmetic  10.9 us (6%)
  starting transfers between devices  10.7 us (6%)
  local copies, waits for them, and re-layouts  8.06 us (4%)
    all_gather x1, blocking collectives, local(): every = lax.all_gather(part, ('dp', 'ctx', 'tp'))  63.8 us
    all_to_all x1, blocking collectives, local(): lax.all_to_all(spread(packed), ('ctx', 'tp'), split_axis=0, concat_axis=0...  21.8 us
    all_gather x1, blocking collectives, local(): gate_all = lax.all_gather(gate_own, 'dp')  21 us
    dot_general x2, matrix products, project(): lax.dot_general(value, down_weight, (((1,), (1,)), ((), ())), preferred_e...  17.6 us
    ppermute x6, waiting for transfers between devices, swap(): return lax.ppermute(value, 'dp', [(i, i ^ distance) for i in range(count)])  13.6 us
    dot_general x1, matrix products, local(): lax.dot_general(saved, weighted, (((0,), (0,)), ((), ())), preferred_elem...  11.4 us
    reduce_sum x2, other arithmetic, parts(): return jnp.sum(left.astype(jnp.float32) * right.astype(jnp.float32), axis=1)  6.42 us
    all_to_all x1, waiting for transfers between devices, local(): rows = lax.all_to_all(rows, 'dp', split_axis=0, concat_axis=0, tiled=True)  6.18 us
  transfers between devices with their start and end apart: 8, of which 3 were waited for; matrix products, arithmetic and copies ran while one was open for 21% of the time, Pallas kernels for 0%

profile of v1, /device:TPU:0, one launch (start us, length us, event | category | flops | bytes accessed | tf_op | source)
XLA Modules:
  0.0 190.6 jit_solution(8914961434303346431)
XLA Ops:
  0.6 0.8 copy.42
  1.5 0.1 reshape.106
  1.6 0.2 fusion.13
  1.8 0.1 convert_element_type.130
  2.0 0.7 multiply_add_fusion
  2.8 0.3 convolution_convert_fusion.3
  3.2 21.8 %all_to_all.15 = bf16[8,36,768]{2,1,0:T(8,128)(2,1)S(1)} all-to-all(bf16[8,36,768]{2,1,0:T(8,128)(2,1)S(1)} %reshape_reshape.6), channel_id=1, replica_groups=mesh['dp'=4,'ctx'=2,'tp'=4] {'ctx','tp'}, dimensions={0} | all-to-all | bytes 884736 | tf_op jit(solution)/shard_map/all_to_all | solution.py:62
  24.9 0.2 copy.47
  25.1 0.8 copy.48
  25.9 3.5 %all-to-all-start.2 = ((bf16[4,72,768]{2,1,0:T(8,128)(2,1)}), bf16[4,72,768]{2,1,0:T(8,128)(2,1)S(1)}, u32[]{:S(2)}, u32[]{:S(2)}) async-start(bf16[4,72,768]{2,1,0:T(8,128)(2,1)} %copy.48), calls=%async_computation.2 | async-start | bytes 884736 | tf_op jit(solution)/shard_map/all_to_all | solution.py:70
  29.4 2.0 %collective-permute-start.4 = (bf16[72,8192]{1,0:T(8,128)(2,1)}, bf16[72,8192]{1,0:T(8,128)(2,1)}, u32[]{:S(2)}, u32[]{:S(2)}) collective-permute-start(bf16[72,8192]{1,0:T(8,128)(2,1)} %param.8), channel_id=1, source_target_pairs={{0,16},{8,24},{16,0},{24,8},{1,17},{9,25},{17,1},{25,9},{2,18},{10... | collective-permute-start | bytes 3538952 | tf_op jit(solution)/shard_map/ppermute | solution.py:12
  31.6 6.2 %all-to-all-done.2 = bf16[4,72,768]{2,1,0:T(8,128)(2,1)S(1)} async-done(((bf16[4,72,768]{2,1,0:T(8,128)(2,1)}), bf16[4,72,768]{2,1,0:T(8,128)(2,1)S(1)}, u32[]{:S(2)}, u32[]{:S(2)}) %all-to-all-start.2) | async-done | bytes 442400 | tf_op jit(solution)/shard_map/all_to_all | solution.py:70
  37.8 8.8 %convolution_convert_fusion.1 = bf16[144,8192]{1,0:T(8,128)(2,1)S(1)} fusion(bf16[8192,768]{1,0:T(8,128)(2,1)} %param.9, bf16[72,768]{1,0:T(8,128)(2,1)S(1)} %get-tuple-element.26, bf16[72,768]{1,0:T(8,128)(2,1)S(1)} %get-tuple-element.27), kind=kOutput, calls=%fused_computation.1 | convolution fusion | flops 1813561344 | bytes 15163392 | tf_op jit(solution)/shard_map/dot_general | solution.py:80
  46.6 1.4 copy-done.1
  48.0 1.1 slice.28
  49.1 13.6 %collective-permute-done.4 = bf16[72,8192]{1,0:T(8,128)(2,1)} collective-permute-done((bf16[72,8192]{1,0:T(8,128)(2,1)}, bf16[72,8192]{1,0:T(8,128)(2,1)}, u32[]{:S(2)}, u32[]{:S(2)}) %collective-permute-start.4) | collective-permute-done | bytes 1179680 | tf_op jit(solution)/shard_map/ppermute | solution.py:12
  62.7 0.1 reshape.111
  62.8 8.8 %convolution_convert_fusion.2 = bf16[144,8192]{1,0:T(8,128)(2,1)S(1)} fusion(bf16[8192,768]{1,0:T(8,128)(2,1)} %param.9, bf16[72,768]{1,0:T(8,128)(2,1)S(1)} %get-tuple-element.28, bf16[72,768]{1,0:T(8,128)(2,1)S(1)} %get-tuple-element.25), kind=kOutput, calls=%fused_computation.2 | convolution fusion | flops 1813561344 | bytes 15163392 | tf_op jit(solution)/shard_map/dot_general | solution.py:80
  71.6 1.1 slice.26
  72.7 0.5 collective-permute-start
  73.2 2.5 %fusion.10 = (f32[72]{0:T(128)S(1)}, f32[72]{0:T(128)S(1)}) fusion(bf16[72,8192]{1,0:T(8,128)(2,1)} %param.8, bf16[144,8192]{1,0:T(8,128)(2,1)S(1)} %convolution_convert_fusion.2, bf16[72,8192]{1,0:T(8,128)(2,1)} %collective-permute-done.3), kind=kLoop, calls=%fused_computation.17 | loop fusion | flops 4718448 | bytes 4719168 | tf_op jit(solution)/shard_map/reduce_sum | solution.py:100
  75.8 3.9 %fusion.12 = (f32[72]{0:T(128)S(1)}, f32[72]{0:T(128)S(1)}, bf16[72,8192]{1,0:T(8,128)(2,1)}) fusion(bf16[72,8192]{1,0:T(8,128)(2,1)} %collective-permute-done.4, bf16[144,8192]{1,0:T(8,128)(2,1)S(1)} %copy-done.2, bf16[72,8192]{1,0:T(8,128)(2,1)} %collective-permute-done.5, bf16[72,8192]{1,0:T(8,128)(2,1)} %collective-permute-done.1), kind=kLoop, calls=%fused_computation.19 | loop fusion | flops 6487920 | bytes 7078464 | tf_op jit(solution)/shard_map/reduce_sum | solution.py:100
  79.7 63.8 %all-gather.2 = f32[32,4,72]{2,1,0:T(4,128)S(1)} all-gather(f32[1,4,72]{2,1,0:T(4,128)S(1)} %maximum_bitcast_fusion), channel_id=2, replica_groups=mesh['dp'=4,'ctx'=2,'tp'=4] {'dp','ctx','tp'}, dimensions={0}, use_global_device_ids=true | all-gather | bytes 38016 | tf_op jit(solution)/shard_map/all_gather | solution.py:111
  143.8 0.2 select_reduce_fusion
  144.0 0.7 convert_element_type.155
  144.7 3.6 %all-to-all-start = ((bf16[8,36,1]{1,2,0:T(2,128)(2,1)}), bf16[8,36,1]{1,2,0:T(2,128)(2,1)S(1)}, u32[]{:S(2)}, u32[]{:S(2)}) async-start(bf16[8,36,1]{1,2,0:T(2,128)(2,1)} %convert_element_type.155), calls=%async_computation | async-start | bytes 8192 | tf_op jit(solution)/shard_map/all_to_all | solution.py:63
  148.6 0.6 copy.49
  149.3 1.2 collective-permute-start.2
  150.4 4.2 %all-to-all-done = bf16[8,36,1]{1,2,0:T(2,128)(2,1)S(1)} async-done(((bf16[8,36,1]{1,2,0:T(2,128)(2,1)}), bf16[8,36,1]{1,2,0:T(2,128)(2,1)S(1)}, u32[]{:S(2)}, u32[]{:S(2)}) %all-to-all-start) | async-done | bytes 608 | tf_op jit(solution)/shard_map/all_to_all | solution.py:63
  154.9 21.0 %all-gather.1 = bf16[4,1,72]{2,1,0:T(2,128)(2,1)S(1)} all-gather(bf16[1,1,72]{2,1,0:T(2,128)(2,1)S(1)} %reshape.115), channel_id=1, replica_groups=mesh['dp'=4,'ctx'=2,'tp'=4] {'dp'}, dimensions={0}, use_global_device_ids=true | all-gather | bytes 720 | tf_op jit(solution)/shard_map/all_gather | solution.py:71
  176.0 11.4 %convolution_convert_fusion = bf16[8192,768]{1,0:T(8,128)(2,1)} fusion(bf16[72,8192]{1,0:T(8,128)(2,1)} %collective-permute-done.5, bf16[72,8192]{1,0:T(8,128)(2,1)} %collective-permute-done.4, bf16[72,8192]{1,0:T(8,128)(2,1)} %collective-permute-done.3, bf16[72,8192]{1,0:T(8,128)(2,1)} %param.8, bf16[72,768]{1,0:T(8,128)(2,1)S(1)} %get-tuple-element.26, ...), kind=kOutput, calls=%fused_computation | convolution fusion | flops 3651256320 | bytes 17745024 | tf_op jit(solution)/shard_map/dot_general | solution.py:95
  187.4 3.1 %fusion.9 = bf16[72,8192]{1,0:T(8,128)(2,1)} fusion(bf16[72,8192]{1,0:T(8,128)(2,1)} %collective-permute-done.2, bf16[72,8192]{1,0:T(8,128)(2,1)} %collective-permute-done, f32[72]{0:T(128)S(1)} %reshape.112, bf16[144,8192]{1,0:T(8,128)(2,1)S(1)} %convolution_convert_fusion.2), kind=kLoop, calls=%fused_computation.16 | loop fusion | flops 4128768 | bytes 4718880 | tf_op jit(solution)/shard_map/convert_element_type | solution.py:122
  (40 shorter events, 1.4 us)
Async XLA Ops:
  0.6 2.1 %copy-start = (bf16[128,768]{1,0:T(8,128)(2,1)S(1)}, bf16[128,768]{1,0:T(8,128)(2,1)}, u32[]{:S(2)}) copy-start(bf16[128,768]{1,0:T(8,128)(2,1)} %param.5) | copy-start | bytes 589828
  3.1 28.3 %copy-start.3 = (f32[128,2]{0,1:T(2,128)S(1)}, f32[128,2]{0,1:T(2,128)}, u32[]{:S(2)}) copy-start(f32[128,2]{0,1:T(2,128)} %param.6) | copy-start | bytes 3076
  25.9 11.9 %all-to-all-start.2 = ((bf16[4,72,768]{2,1,0:T(8,128)(2,1)}), bf16[4,72,768]{2,1,0:T(8,128)(2,1)S(1)}, u32[]{:S(2)}, u32[]{:S(2)}) async-start(bf16[4,72,768]{2,1,0:T(8,128)(2,1)} %copy.48), calls=%async_computation.2 | async-start | bytes 884736 | tf_op jit(solution)/shard_map/all_to_all | solution.py:70
  29.4 33.3 %collective-permute-start.4 = (bf16[72,8192]{1,0:T(8,128)(2,1)}, bf16[72,8192]{1,0:T(8,128)(2,1)}, u32[]{:S(2)}, u32[]{:S(2)}) collective-permute-start(bf16[72,8192]{1,0:T(8,128)(2,1)} %param.8), channel_id=1, source_target_pairs={{0,16},{8,24},{16,0},{24,8},{1,17},{9,25},{17,1},{25,9},{2,18},{10... | collective-permute-start | bytes 3538952 | tf_op jit(solution)/shard_map/ppermute | solution.py:12
  31.4 41.9 %collective-permute-start.3 = (bf16[72,8192]{1,0:T(8,128)(2,1)}, bf16[72,8192]{1,0:T(8,128)(2,1)}, u32[]{:S(2)}, u32[]{:S(2)}) collective-permute-start(bf16[72,8192]{1,0:T(8,128)(2,1)} %param.8), channel_id=1, source_target_pairs={{0,8},{8,0},{16,24},{24,16},{1,9},{9,1},{17,25},{25,17},{2,10},{10... | collective-permute-start | bytes 3538952 | tf_op jit(solution)/shard_map/ppermute | solution.py:12
  46.6 1.4 copy-start.1
  49.1 26.6 %collective-permute-start.1 = (bf16[72,8192]{1,0:T(8,128)(2,1)}, bf16[72,8192]{1,0:T(8,128)(2,1)}, u32[]{:S(2)}, u32[]{:S(2)}) collective-permute-start(bf16[72,8192]{1,0:T(8,128)(2,1)} %slice.28), channel_id=1, source_target_pairs={{0,8},{8,0},{16,24},{24,16},{1,9},{9,1},{17,25},{25,17},{2,10},{10... | collective-permute-start | bytes 3538952 | tf_op jit(solution)/shard_map/ppermute | solution.py:12
  62.7 13.1 %collective-permute-start.5 = (bf16[72,8192]{1,0:T(8,128)(2,1)}, bf16[72,8192]{1,0:T(8,128)(2,1)}, u32[]{:S(2)}, u32[]{:S(2)}) collective-permute-start(bf16[72,8192]{1,0:T(8,128)(2,1)} %collective-permute-done.4), channel_id=1, source_target_pairs={{0,8},{8,0},{16,24},{24,16},{1,9},{9,1},{17,25},{25,17},{2,10},{10... | collective-permute-start | bytes 3538952 | tf_op jit(solution)/shard_map/ppermute | solution.py:12
  72.7 3.1 %copy-start.2 = (bf16[144,8192]{1,0:T(8,128)(2,1)S(1)}, bf16[144,8192]{1,0:T(8,128)(2,1)}, u32[]{:S(2)}) copy-start(bf16[144,8192]{1,0:T(8,128)(2,1)} %copy-done.1) | copy-start | bytes 7077892
  72.7 114.7 %collective-permute-start = (bf16[72,8192]{1,0:T(8,128)(2,1)}, bf16[72,8192]{1,0:T(8,128)(2,1)}, u32[]{:S(2)}, u32[]{:S(2)}) collective-permute-start(bf16[72,8192]{1,0:T(8,128)(2,1)} %slice.26), channel_id=1, source_target_pairs={{0,8},{8,0},{16,24},{24,16},{1,9},{9,1},{17,25},{25,17},{2,10},{10... | collective-permute-start | bytes 3538952 | tf_op jit(solution)/shard_map/ppermute | solution.py:12
  144.7 9.9 %all-to-all-start = ((bf16[8,36,1]{1,2,0:T(2,128)(2,1)}), bf16[8,36,1]{1,2,0:T(2,128)(2,1)S(1)}, u32[]{:S(2)}, u32[]{:S(2)}) async-start(bf16[8,36,1]{1,2,0:T(2,128)(2,1)} %convert_element_type.155), calls=%async_computation | async-start | bytes 8192 | tf_op jit(solution)/shard_map/all_to_all | solution.py:63
  149.3 38.1 %collective-permute-start.2 = (bf16[72,8192]{1,0:T(8,128)(2,1)}, bf16[72,8192]{1,0:T(8,128)(2,1)}, u32[]{:S(2)}, u32[]{:S(2)}) collective-permute-start(bf16[72,8192]{1,0:T(8,128)(2,1)} %get-tuple-element.24), channel_id=1, source_target_pairs={{0,16},{8,24},{16,0},{24,8},{1,17},{9,25},{17,1},{25,9},{2,18},{10... | collective-permute-start | bytes 3538952 | tf_op jit(solution)/shard_map/ppermute | solution.py:12

commit v2 on v1

v2 whole, which is shorter than its diff:
```python
import functools

import jax
import jax.numpy as jnp
from jax import lax
from jax.experimental import pallas as pl
from jax.experimental.pallas import tpu as pltpu
from jax.sharding import PartitionSpec as P

EXPERTS = 8
TOP = 2
LANES = 128
MESH = pl.DeviceIdType.MESH


def swap(value, distance):
    count = lax.axis_size("dp")
    return lax.ppermute(value, "dp", [(i, i ^ distance) for i in range(count)])


def exchange(
    sizes,
    packed,
    pick,
    pick_gate,
    slot_lane,
    saved_in,
    weight_in,
    far_sum,
    near_sum,
    saved,
    weighted,
    gate_out,
    part,
    recv,
    weight,
    rows,
    far_own,
    far_stage,
    near_stage,
    far_in,
    near_in,
    disp_send,
    disp_recv,
    cross_send,
    cross_recv,
    core_send,
    core_recv,
    pass_send,
    pass_recv,
    far_send,
    far_recv,
    near_send,
    near_recv,
    weight_sem,
    own_sem,
):
    dp_count, context_count, tensor_count, group_size = sizes
    block_count = context_count * tensor_count
    source_count = dp_count * context_count
    slots = saved.shape[1]
    hidden = saved.shape[2]
    width = min(1024, hidden)
    chunks = hidden // width
    pad = packed.shape[1]
    me = lax.axis_index("dp")
    ctx = lax.axis_index("ctx")
    tp = lax.axis_index("tp")
    mate = me + 1 - 2 * (me % 2)
    cross = me + 2 - 4 * ((me // 2) % 2)
    order = (me, mate, cross, cross + 1 - 2 * (cross % 2))
    block = ctx * tensor_count + tp
    source = me * context_count + ctx
    to_self = tp == me

    def piece(k):
        return pl.ds(pl.multiple_of(k * width, width), width)

    def load(k):
        return pltpu.make_async_copy(
            weight_in.at[piece(k), :], weight.at[piece(k), :], weight_sem.at[k]
        )

    own = pltpu.make_async_copy(saved_in, saved.at[0], own_sem)

    @pl.loop(0, chunks)
    def _(k):
        load(k).start()

    own.start()

    barrier = pltpu.get_barrier_semaphore()

    @pl.loop(0, source_count)
    def _(n):
        @pl.when(jnp.logical_not(to_self & (n == source)))
        def _():
            pl.semaphore_signal(
                barrier,
                inc=1,
                device_id=(n // context_count, n % context_count, me),
                device_id_type=MESH,
            )

    for other in (mate, cross):
        pl.semaphore_signal(barrier, inc=1, device_id=(other, ctx, tp), device_id_type=MESH)

    @pl.when(to_self)
    def _():
        pl.semaphore_wait(barrier, block_count + 1)

    @pl.when(jnp.logical_not(to_self))
    def _():
        pl.semaphore_wait(barrier, block_count + 2)

    def dispatch(b):
        return pltpu.make_async_remote_copy(
            src_ref=packed.at[b // group_size],
            dst_ref=recv.at[source],
            send_sem=disp_send.at[b],
            recv_sem=disp_recv.at[source],
            device_id=(tp, b // tensor_count, b % tensor_count),
            device_id_type=MESH,
        )

    def arrival(n):
        return pltpu.make_async_remote_copy(
            src_ref=packed.at[0],
            dst_ref=recv.at[n],
            send_sem=disp_send.at[0],
            recv_sem=disp_recv.at[n],
            device_id=(tp, ctx, tp),
            device_id_type=MESH,
        )

    def remote(src, dst, send, recv_sem, k, device):
        return pltpu.make_async_remote_copy(
            src_ref=src,
            dst_ref=dst,
            send_sem=send.at[k],
            recv_sem=recv_sem.at[k],
            device_id=(device, ctx, tp),
            device_id_type=MESH,
        )

    def to_cross(k):
        return remote(
            saved_in.at[:, piece(k)], saved.at[2, :, piece(k)], cross_send, cross_recv, k, cross
        )

    def to_core(k):
        return remote(
            saved_in.at[:, piece(k)], saved.at[1, :, piece(k)], core_send, core_recv, k, mate
        )

    def pass_on(k):
        return remote(
            saved.at[2, :, piece(k)], saved.at[3, :, piece(k)], pass_send, pass_recv, k, mate
        )

    def send_far(k):
        return remote(
            far_stage.at[:, piece(k)], far_in.at[:, piece(k)], far_send, far_recv, k, mate
        )

    def send_near(k):
        return remote(
            near_stage.at[:, piece(k)], near_in.at[:, piece(k)], near_send, near_recv, k, mate
        )

    @pl.loop(0, block_count)
    def _(b):
        @pl.when(jnp.logical_not(to_self & (b == block)))
        def _():
            dispatch(b).start()

    @pl.loop(0, chunks)
    def _(k):
        to_cross(k).start()

    @pl.loop(0, chunks)
    def _(k):
        to_core(k).start()

    @pl.when(to_self)
    def _():
        recv[source] = packed[block // group_size]

    part[...] = jnp.zeros_like(part)

    @pl.loop(0, source_count)
    def _(n):
        @pl.when(jnp.logical_not(to_self & (n == source)))
        def _():
            arrival(n).wait_recv()

    placed, gate_columns = [], []
    for sequence in order:
        found = recv[pl.ds(sequence * context_count, context_count)]
        found = found.reshape(context_count * pad, found.shape[2])
        placed.append(jnp.dot(pick[...], found, preferred_element_type=jnp.float32))
        gate_lanes = jnp.dot(
            pick_gate[...], found[:, :LANES], preferred_element_type=jnp.float32
        )
        gate_columns.append(jnp.sum(gate_lanes * slot_lane[...], axis=1, keepdims=True))
    row_values = jnp.concatenate(placed, axis=0)
    gate_column = jnp.concatenate(gate_columns, axis=0)
    rows[...] = row_values.astype(jnp.bfloat16)
    weighted[...] = (gate_column * row_values).astype(jnp.bfloat16)
    gate_out[...] = jnp.broadcast_to(gate_columns[0], gate_out.shape)

    @pl.loop(0, chunks)
    def _(k):
        load(k).wait()
        proj = lax.dot_general(
            rows[...],
            weight[piece(k), :],
            (((1,), (1,)), ((), ())),
            preferred_element_type=jnp.float32,
        )
        near_sum[:, piece(k)] = proj[:slots]
        near_stage[:, piece(k)] = proj[slots : 2 * slots].astype(jnp.bfloat16)
        far_own[:, piece(k)] = proj[2 * slots : 3 * slots]
        far_stage[:, piece(k)] = proj[3 * slots :].astype(jnp.bfloat16)
        send_far(k).start()
        send_near(k).start()

    own.wait()

    def tally(m, left, right):
        product = left.astype(jnp.float32) * right.astype(jnp.float32)
        total = product[:, :LANES]
        for j in range(1, width // LANES):
            total = total + product[:, j * LANES : (j + 1) * LANES]
        part[m] += total

    @pl.loop(0, chunks)
    def _(k):
        to_cross(k).wait_recv()
        pass_on(k).start()
        to_core(k).wait_recv()
        tally(0, saved[0, :, piece(k)], near_sum[:, piece(k)])
        tally(1, saved[1, :, piece(k)], near_stage[:, piece(k)])
        tally(2, saved[2, :, piece(k)], far_own[:, piece(k)])
        send_far(k).wait_recv()
        far_sum[:, piece(k)] = (
            far_own[:, piece(k)] + far_in[:, piece(k)].astype(jnp.float32)
        ).astype(jnp.bfloat16)
        send_near(k).wait_recv()
        near_sum[:, piece(k)] += near_in[:, piece(k)].astype(jnp.float32)

    @pl.loop(0, chunks)
    def _(k):
        pass_on(k).wait_recv()
        tally(3, saved[3, :, piece(k)], far_stage[:, piece(k)])

    @pl.loop(0, chunks)
    def _(k):
        to_cross(k).wait_send()
        to_core(k).wait_send()
        pass_on(k).wait_send()
        send_far(k).wait_send()
        send_near(k).wait_send()

    @pl.loop(0, block_count)
    def _(b):
        @pl.when(jnp.logical_not(to_self & (b == block)))
        def _():
            dispatch(b).wait_send()


def run_exchange(packed, pick, pick_gate, slot_lane, hidden_saved, down_weight):
    dp_count = lax.axis_size("dp")
    context_count = lax.axis_size("ctx")
    tensor_count = lax.axis_size("tp")
    block_count = context_count * tensor_count
    slots, hidden = hidden_saved.shape
    cols = down_weight.shape[1]
    chunks = hidden // min(1024, hidden)
    bf16, f32 = jnp.bfloat16, jnp.float32
    vmem = pl.BlockSpec(memory_space=pltpu.VMEM)
    dma = pltpu.SemaphoreType.DMA
    return pl.pallas_call(
        functools.partial(
            exchange, (dp_count, context_count, tensor_count, block_count // EXPERTS)
        ),
        out_shape=[
            jax.ShapeDtypeStruct((slots, hidden), bf16),
            jax.ShapeDtypeStruct((slots, hidden), f32),
            jax.ShapeDtypeStruct((4, slots, hidden), bf16),
            jax.ShapeDtypeStruct((4 * slots, cols), bf16),
            jax.ShapeDtypeStruct((slots, LANES), f32),
            jax.ShapeDtypeStruct((4, slots, LANES), f32),
        ],
        in_specs=[vmem] * 4 + [pl.BlockSpec(memory_space=pl.ANY)] * 2,
        out_specs=[vmem] * 6,
        scratch_shapes=[
            pltpu.VMEM((dp_count * context_count,) + packed.shape[1:], bf16),
            pltpu.VMEM((hidden, cols), bf16),
            pltpu.VMEM((4 * slots, cols), bf16),
            pltpu.VMEM((slots, hidden), f32),
            pltpu.VMEM((slots, hidden), bf16),
            pltpu.VMEM((slots, hidden), bf16),
            pltpu.VMEM((slots, hidden), bf16),
            pltpu.VMEM((slots, hidden), bf16),
            dma((block_count,)),
            dma((dp_count * context_count,)),
        ]
        + [dma((chunks,))] * 11
        + [dma],
        compiler_params=pltpu.CompilerParams(
            collective_id=0, has_side_effects=True, vmem_limit_bytes=56 * 1024 * 1024
        ),
        cost_estimate=pl.CostEstimate(
            flops=8 * slots * hidden * cols, bytes_accessed=2 * hidden * cols, transcendentals=0
        ),
    )(packed, pick, pick_gate, slot_lane, hidden_saved, down_weight)


def local(upstream, router_logits, expert_ids, hidden_saved, down_weight):
    token_count, feature_cols = upstream.shape
    dp_count = lax.axis_size("dp")
    tensor_count = lax.axis_size("tp")
    context_count = lax.axis_size("ctx")
    block_count = context_count * tensor_count
    slots = hidden_saved.shape[0]
    capacity = slots // context_count
    group_size = block_count // EXPERTS
    pad = -(-(capacity + 1) // 16) * 16
    me = lax.axis_index("dp")
    assert dp_count == 4 and tensor_count == dp_count and capacity <= LANES

    gates = 1.0 / (1.0 + jnp.exp(router_logits[:, ::-1] - router_logits))
    gates_sent = gates.astype(jnp.bfloat16)
    routes = expert_ids.reshape(-1)
    onehot = routes[:, None] == jnp.arange(EXPERTS, dtype=jnp.int32)[None, :]
    number = jnp.arange(token_count * TOP, dtype=jnp.int32)
    earlier = lax.dot_general(
        (number[:, None] > number[None, :]).astype(jnp.bfloat16),
        onehot.astype(jnp.bfloat16),
        (((1,), (0,)), ((), ())),
        preferred_element_type=jnp.float32,
    )
    slot = jnp.sum(jnp.where(onehot, earlier, 0.0), axis=1).astype(jnp.int32)
    position = routes * pad + slot
    place = (position[:, None] == jnp.arange(EXPERTS * pad, dtype=jnp.int32)[None, :]).astype(
        jnp.float32
    )
    token_place = place.reshape(token_count, TOP, EXPERTS * pad).sum(axis=1).astype(jnp.bfloat16)
    gate_packed = jnp.sum(place * gates_sent.reshape(-1).astype(jnp.float32)[:, None], axis=0)
    packed = lax.dot_general(
        token_place, upstream, (((0,), (0,)), ((), ())), preferred_element_type=jnp.float32
    ).reshape(EXPERTS, pad, feature_cols)
    gate_line = jnp.pad(
        gate_packed.reshape(EXPERTS, 1, pad), ((0, 0), (0, 0), (0, feature_cols - pad))
    )
    line = jnp.arange(pad, dtype=jnp.int32)[None, :, None]
    packed = jnp.where(line == capacity, gate_line, packed).astype(jnp.bfloat16)

    index = jnp.arange(slots, dtype=jnp.int32)
    first = (index // capacity) * pad
    columns = jnp.arange(context_count * pad, dtype=jnp.int32)[None, :]
    pick = ((first + index % capacity)[:, None] == columns).astype(jnp.bfloat16)
    pick_gate = ((first + capacity)[:, None] == columns).astype(jnp.bfloat16)
    slot_lane = (
        (index % capacity)[:, None] == jnp.arange(LANES, dtype=jnp.int32)[None, :]
    ).astype(jnp.float32)

    far_sum, near_sum, saved, weighted, gate_own, part = run_exchange(
        packed, pick, pick_gate, slot_lane, hidden_saved, down_weight
    )
    cross = swap(far_sum, 2)

    part = part.sum(axis=2)
    order = jnp.stack([me ^ m for m in range(4)])
    part = jnp.stack([jnp.sum(jnp.where((order == s)[:, None], part, 0.0), 0) for s in range(4)])
    part = lax.all_to_all(part, "dp", split_axis=0, concat_axis=0, tiled=True).sum(axis=0)
    outgoing = jnp.broadcast_to(
        part.reshape(context_count, 1, capacity), (context_count, tensor_count, capacity)
    ).reshape(block_count, capacity)
    returned = lax.all_to_all(outgoing, ("ctx", "tp"), split_axis=0, concat_axis=0, tiled=True)
    expert_sums = returned.reshape(EXPERTS, group_size, capacity).sum(axis=1)
    expert_sums = jnp.pad(expert_sums, ((0, 0), (0, pad - capacity))).reshape(-1)
    route_grad = jnp.sum(place * expert_sums[None, :], axis=1).reshape(token_count, TOP)
    logit_grad = gates * (route_grad - jnp.sum(gates * route_grad, axis=1, keepdims=True))

    down_grad = lax.dot_general(
        saved.reshape(4 * slots, -1),
        weighted,
        (((0,), (0,)), ((), ())),
        preferred_element_type=jnp.float32,
    ).astype(jnp.bfloat16)

    proj = near_sum + cross.astype(jnp.float32)
    hidden_grad = (gate_own[:, :1] * proj).astype(jnp.bfloat16)
    return (hidden_grad, down_grad, logit_grad)


def solution(mesh):
    in_specs = (
        P(("dp", "ctx"), "tp"),
        P(("dp", "ctx"), None),
        P(("dp", "ctx"), None),
        P("dp", ("ctx", "tp")),
        P(("ctx", "tp"), "dp"),
    )
    out_specs = (P("dp", ("ctx", "tp")), P(("ctx", "tp"), "dp"), P(("dp", "ctx"), None))
    return jax.shard_map(local, mesh=mesh, in_specs=in_specs, out_specs=out_specs, check_vma=False)
```

time: 191 us -> 90.1 us (0.47)
  blocking collectives: 107 us -> 0 us
  Pallas kernels: 0 us -> 46.3 us
  matrix products: 29.5 us -> 12.1 us
  waiting for transfers between devices: 24 us -> 9.82 us
  local copies, waits for them, and re-layouts: 8.06 us -> 3.91 us
  other arithmetic: 10.9 us -> 8.27 us
  starting transfers between devices: 10.7 us -> 8.52 us
    all_gather x2 -> x0, blocking collectives: 84.8 us -> none  [the longest x1 63.8 us: local(): every = lax.all_gather(part, ('dp', 'ctx', 'tp'))]
    pallas_call x0 -> x1, Pallas kernels: none -> 46.3 us  [run_exchange(): pl.pallas_call(functools.partial(exchange, (dp_count, context_count, tens...]
    all_to_all x1 -> x0, blocking collectives: 21.8 us -> none  [local(): lax.all_to_all(spread(packed), ('ctx', 'tp'), split_axis=0, concat_axis=0...]
    dot_general x3 -> x1, matrix products: 29 us -> 11.5 us  [local(): lax.dot_general(saved.reshape(4 * slots, -1), weighted, (((0,), (0,)), ((...]
    ppermute x6 -> x1, waiting for transfers between devices: 13.6 us -> 3.61 us  [swap(): return lax.ppermute(value, 'dp', [(i, i ^ distance) for i in range(count)])]
    reduce_sum x4 -> x5, other arithmetic: 6.49 us -> 1.43 us  [the longest x1 1.05 us: local(): part = part.sum(axis=2)]
    all_to_all x2, waiting for transfers between devices: 10.4 us -> 6.22 us  [the longest x1 6.21 us: local(): lax.all_to_all(outgoing, ('ctx', 'tp'), split_axis=0, concat_axis=0, tile...]
    slice x3 -> x1, local copies, waits for them, and re-layouts: 2.2 us -> 0.1 us  [local(): hidden_grad = (gate_own[:, :1] * proj).astype(jnp.bfloat16)]
  transfers between devices with their start and end apart: 8 -> 3, of which waited for: 3 -> 2; matrix products, arithmetic and copies ran while one was open for 21% -> 15% of each run, Pallas kernels for 0% -> 0%
where the time goes in v2:
time: 90.1 us; the launch traced here: 89.8 us
  Pallas kernels  46.3 us (51%)
  matrix products  12.1 us (13%)
  waiting for transfers between devices  9.82 us (11%)
  starting transfers between devices  8.52 us (9%)
  other arithmetic  8.27 us (9%)
  local copies, waits for them, and re-layouts  3.91 us (4%)
    pallas_call x1, Pallas kernels, run_exchange(): pl.pallas_call(functools.partial(exchange, (dp_count, context_count, tens...  46.3 us
    dot_general x1, matrix products, local(): lax.dot_general(saved.reshape(4 * slots, -1), weighted, (((0,), (0,)), ((...  11.5 us
    all_to_all x1, waiting for transfers between devices, local(): lax.all_to_all(outgoing, ('ctx', 'tp'), split_axis=0, concat_axis=0, tile...  6.21 us
    ppermute x1, waiting for transfers between devices, swap(): return lax.ppermute(value, 'dp', [(i, i ^ distance) for i in range(count)])  3.61 us
    all_to_all x1, starting transfers between devices, local(): lax.all_to_all(outgoing, ('ctx', 'tp'), split_axis=0, concat_axis=0, tile...  3.31 us
    all_to_all x1, starting transfers between devices, local(): lax.all_to_all(part, 'dp', split_axis=0, concat_axis=0, tiled=True)  3.22 us
    convert_element_type x1, other arithmetic, local(): hidden_grad = (gate_own[:, :1] * proj).astype(jnp.bfloat16)  2.64 us
    unnamed x9, local copies, waits for them, and re-layouts  2.26 us
  transfers between devices with their start and end apart: 3, of which 2 were waited for; matrix products, arithmetic and copies ran while one was open for 15% of the time, Pallas kernels for 0%

profile of v2, /device:TPU:0, one launch (start us, length us, event | category | flops | bytes accessed | tf_op | source)
XLA Modules:
  0.0 89.8 jit_solution(1555396870866521796)
XLA Ops:
  0.7 0.8 copy.30
  1.5 0.1 reshape.225
  1.7 0.2 fusion
  2.0 0.7 fusion.5.slot_lane
  2.7 0.8 copy.31
  3.6 0.1 reshape.230
  3.7 0.2 select_reduce_fusion.1
  3.9 0.1 reshape.226
  4.0 0.1 convert_element_type.62
  4.2 0.7 multiply_add_fusion
  4.9 0.1 convert_reduce_fusion
  5.0 0.7 fusion.3
  5.7 0.3 fusion.9
  6.1 0.9 %select_convert_fusion.packed = bf16[8,48,768]{2,1,0:T(8,128)(2,1)} fusion(bf16[8,48,768]{2,1,0:T(8,128)(2,1)S(1)} %bitcast.21, bf16[8,768]{1,0:T(8,128)(2,1)S(1)} %pad_bitcast_fusion, pred[48]{0:T(512)(128)(4,1)S(1)} %iota_compare_fusion.9), kind=kLoop, calls=%fused_computation.2 | loop fusion | flops 294912 | bytes 1191984 | tf_op jit(solution)/shard_map/convert_element_type | solution.py:358
  7.0 46.3 %shard_map.76 = (bf16[72,8192]{1,0:T(8,128)(2,1)}, f32[72,8192]{1,0:T(8,128)}, bf16[4,72,8192]{2,1,0:T(8,128)(2,1)}, bf16[288,768]{1,0:T(8,128)(2,1)}, f32[72,128]{1,0:T(8,128)}, /*index=5*/f32[4,72,128]{2,1,0:T(8,128)}) custom-call(bf16[8,48,768]{2,1,0:T(8,128)(2,1)} %select_convert_fusion.packed, bf16[72,96]{1,0:T(8,128)(2,1)} %get-tuple-element.36.pick, ...), custom_call_target="tpu_custom_call" | custom-call | flops 3623878656 | bytes 12582912 | tf_op jit(solution)/shard_map/pallas_call | solution.py:283
  53.3 1.0 %reduce_sum.108 = f32[4,72]{1,0:T(4,128)S(1)} reduce(f32[4,72,128]{2,1,0:T(8,128)} %get-tuple-element.14, f32[]{:T(128)} %constant.22.clone.1), dimensions={2}, to_apply=%region_3.4 | reduce | flops 36576 | bytes 148612 | tf_op jit(solution)/shard_map/reduce_sum | solution.py:374
  54.4 0.1 select_reduce_fusion.5
  54.5 0.6 pad_maximum_fusion
  55.1 3.2 %all-to-all-start = ((f32[4,1,72]{2,1,0:T(1,128)}), f32[4,1,72]{2,1,0:T(1,128)S(1)}, u32[]{:S(2)}, u32[]{:S(2)}) async-start(f32[4,1,72]{2,1,0:T(1,128)} %bitcast.12), calls=%async_computation | async-start | bytes 4096 | tf_op jit(solution)/shard_map/all_to_all | solution.py:377
  58.3 2.0 %collective-permute-start = (bf16[72,8192]{1,0:T(8,128)(2,1)}, bf16[72,8192]{1,0:T(8,128)(2,1)}, u32[]{:S(2)}, u32[]{:S(2)}) collective-permute-start(bf16[72,8192]{1,0:T(8,128)(2,1)} %get-tuple-element.11), channel_id=1, source_target_pairs={{0,16},{8,24},{16,0},{24,8},{1,17},{9,25},{17,1},{25,9},{2,18},{10... | collective-permute-start | bytes 3538952 | tf_op jit(solution)/shard_map/ppermute | solution.py:18
  60.3 11.5 %convolution_convert_fusion = bf16[8192,768]{1,0:T(8,128)(2,1)} fusion(bf16[288,8192]{1,0:T(8,128)(2,1)} %bitcast.27, bf16[288,768]{1,0:T(8,128)(2,1)} %get-tuple-element.13), kind=kOutput, calls=%fused_computation | convolution fusion | flops 3630170112 | bytes 17743872 | tf_op jit(solution)/shard_map/dot_general | solution.py:387
  72.0 0.6 broadcast_in_dim.86
  72.6 3.3 %all-to-all-start.1 = ((f32[8,1,36]{2,1,0:T(1,128)}), f32[8,1,36]{2,1,0:T(1,128)S(1)}, u32[]{:S(2)}, u32[]{:S(2)}) async-start(f32[8,1,36]{2,1,0:T(1,128)} %bitcast.13), calls=%async_computation.1 | async-start | bytes 8192 | tf_op jit(solution)/shard_map/all_to_all | solution.py:381
  75.9 0.1 slice_reduce_fusion
  76.0 6.2 %all-to-all-done.1 = f32[8,1,36]{2,1,0:T(1,128)S(1)} async-done(((f32[8,1,36]{2,1,0:T(1,128)}), f32[8,1,36]{2,1,0:T(1,128)S(1)}, u32[]{:S(2)}, u32[]{:S(2)}) %all-to-all-start.1) | async-done | bytes 1184 | tf_op jit(solution)/shard_map/all_to_all | solution.py:381
  82.3 0.2 select_reduce_fusion
  82.5 0.1 reshape.229
  82.6 0.1 multiply_reduce_fusion
  82.8 0.1 subtract_multiply_fusion
  82.9 0.6 copy.35
  83.5 3.6 %collective-permute-done = bf16[72,8192]{1,0:T(8,128)(2,1)} collective-permute-done((bf16[72,8192]{1,0:T(8,128)(2,1)}, bf16[72,8192]{1,0:T(8,128)(2,1)}, u32[]{:S(2)}, u32[]{:S(2)}) %collective-permute-start) | collective-permute-done | bytes 1179680 | tf_op jit(solution)/shard_map/ppermute | solution.py:18
  87.1 2.6 %multiply_convert_fusion = bf16[72,8192]{1,0:T(8,128)(2,1)} fusion(f32[72,8192]{1,0:T(8,128)S(1)} %copy-done.1, bf16[72,8192]{1,0:T(8,128)(2,1)} %collective-permute-done, f32[72]{0:T(128)S(1)} %slice_reduce_fusion), kind=kLoop, calls=%fused_computation.1 | loop fusion | flops 2359296 | bytes 4718880 | tf_op jit(solution)/shard_map/convert_element_type | solution.py:395
  (23 shorter events, 0.5 us)
Async XLA Ops:
  0.6 5.1 %copy-start = (bf16[128,768]{1,0:T(8,128)(2,1)S(1)}, bf16[128,768]{1,0:T(8,128)(2,1)}, u32[]{:S(2)}) copy-start(bf16[128,768]{1,0:T(8,128)(2,1)} %param.5) | copy-start | bytes 589828
  55.1 16.8 %all-to-all-start = ((f32[4,1,72]{2,1,0:T(1,128)}), f32[4,1,72]{2,1,0:T(1,128)S(1)}, u32[]{:S(2)}, u32[]{:S(2)}) async-start(f32[4,1,72]{2,1,0:T(1,128)} %bitcast.12), calls=%async_computation | async-start | bytes 4096 | tf_op jit(solution)/shard_map/all_to_all | solution.py:377
  58.3 28.8 %collective-permute-start = (bf16[72,8192]{1,0:T(8,128)(2,1)}, bf16[72,8192]{1,0:T(8,128)(2,1)}, u32[]{:S(2)}, u32[]{:S(2)}) collective-permute-start(bf16[72,8192]{1,0:T(8,128)(2,1)} %get-tuple-element.11), channel_id=1, source_target_pairs={{0,16},{8,24},{16,0},{24,8},{1,17},{9,25},{17,1},{25,9},{2,18},{10... | collective-permute-start | bytes 3538952 | tf_op jit(solution)/shard_map/ppermute | solution.py:18
  60.3 15.6 %copy-start.2 = (f32[72,128]{1,0:T(8,128)S(1)}, f32[72,128]{1,0:T(8,128)}, u32[]{:S(2)}) copy-start(f32[72,128]{1,0:T(8,128)} %get-tuple-element.9) | copy-start | bytes 110596
  60.3 26.8 %copy-start.1 = (f32[72,8192]{1,0:T(8,128)S(1)}, f32[72,8192]{1,0:T(8,128)}, u32[]{:S(2)}) copy-start(f32[72,8192]{1,0:T(8,128)} %get-tuple-element.10) | copy-start | bytes 7077892
  72.6 9.6 %all-to-all-start.1 = ((f32[8,1,36]{2,1,0:T(1,128)}), f32[8,1,36]{2,1,0:T(1,128)S(1)}, u32[]{:S(2)}, u32[]{:S(2)}) async-start(f32[8,1,36]{2,1,0:T(1,128)} %bitcast.13), calls=%async_computation.1 | async-start | bytes 8192 | tf_op jit(solution)/shard_map/all_to_all | solution.py:381

commit v3 on v2

v3 whole, which is shorter than its diff:
```python
import functools

import jax
import jax.numpy as jnp
import numpy as np
from jax import lax
from jax.experimental import pallas as pl
from jax.experimental.pallas import tpu as pltpu
from jax.sharding import PartitionSpec as P

EXPERTS = 8
TOP = 2
LANES = 128
MESH = pl.DeviceIdType.MESH


def swap(value, distance):
    count = lax.axis_size("dp")
    return lax.ppermute(value, "dp", [(i, i ^ distance) for i in range(count)])


def chunk_width(slots, hidden):
    return min(1024 if slots <= 256 else 128, hidden)


def exchange(
    sizes,
    id_rows,
    logit_rows,
    upstream,
    pick,
    pick_gate,
    slot_lane,
    saved_in,
    weight_in,
    far_sum,
    near_sum,
    saved,
    weighted,
    gate_out,
    part_sum,
    packed,
    recv,
    leaving,
    landing,
    weight,
    rows,
    far_own,
    far_stage,
    near_stage,
    far_in,
    near_in,
    part,
    part_in,
    disp_send,
    disp_recv,
    row_send,
    row_recv,
    part_send,
    part_recv,
    cross_send,
    cross_recv,
    core_send,
    core_recv,
    pass_send,
    pass_recv,
    far_send,
    far_recv,
    near_send,
    near_recv,
    weight_sem,
    own_sem,
):
    context_count, tensor_count, group_size = sizes
    block_count = context_count * tensor_count
    tokens, cols = upstream.shape
    slots = saved.shape[1]
    capacity = slots // context_count
    hidden = saved.shape[2]
    width = chunk_width(slots, hidden)
    chunks = hidden // width
    early = min(3, chunks)
    pad = packed.shape[1]
    me = lax.axis_index("dp")
    ctx = lax.axis_index("ctx")
    tp = lax.axis_index("tp")
    mate = me + 1 - 2 * (me % 2)
    cross = me + 2 - 4 * ((me // 2) % 2)
    order = (me, mate, cross, cross + 1 - 2 * (cross % 2))
    block = ctx * tensor_count + tp

    def piece(k):
        return pl.ds(pl.multiple_of(k * width, width), width)

    def load(k):
        return pltpu.make_async_copy(
            weight_in.at[piece(k), :], weight.at[piece(k), :], weight_sem.at[k]
        )

    own = pltpu.make_async_copy(saved_in, saved.at[0], own_sem)

    barrier = pltpu.get_barrier_semaphore()

    @pl.loop(0, block_count)
    def _(b):
        @pl.when(b != block)
        def _():
            pl.semaphore_signal(
                barrier,
                inc=1,
                device_id=(me, b // tensor_count, b % tensor_count),
                device_id_type=MESH,
            )

    for other in order[1:]:
        pl.semaphore_signal(barrier, inc=1, device_id=(other, ctx, tp), device_id_type=MESH)

    @pl.loop(0, chunks)
    def _(k):
        load(k).start()

    own.start()

    f32, bf16 = jnp.float32, jnp.bfloat16
    token = lax.broadcasted_iota(jnp.int32, (tokens, tokens), 0)
    lane = lax.broadcasted_iota(jnp.int32, (tokens, tokens), 1)
    lane_value = lane.astype(f32)

    def column(line):
        return jnp.sum(jnp.where(token == lane, line, 0.0), axis=1, keepdims=True)

    experts = [column(id_rows[k : k + 1, :].astype(f32)) for k in range(TOP)]
    logits = [column(logit_rows[k : k + 1, :]) for k in range(TOP)]
    gates = [
        (1.0 / (1.0 + jnp.exp(logits[1 - k] - logits[k]))).astype(bf16).astype(f32)
        for k in range(TOP)
    ]
    named = [jnp.where(expert == lane_value, 1.0, 0.0) for expert in experts]
    prior = jnp.dot(
        jnp.where(lane < token, 1.0, 0.0).astype(bf16),
        (named[0] + named[1]).astype(bf16),
        preferred_element_type=f32,
    )
    slot = [jnp.sum(prior * one, axis=1, keepdims=True) for one in named]
    wide = lax.broadcasted_iota(jnp.int32, (tokens, EXPERTS * pad), 1).astype(f32)
    place = sum(
        jnp.where(experts[k] * float(pad) + slot[k] == wide, 1.0, 0.0) for k in range(TOP)
    )
    sorted_rows = lax.dot_general(
        place.astype(bf16), upstream[...], (((0,), (0,)), ((), ())), preferred_element_type=f32
    )
    gate_line = lax.broadcasted_iota(jnp.int32, (pad, LANES), 0) == capacity
    at_slot = [jnp.where(slot[k] == lane_value, gates[k], 0.0) for k in range(TOP)]
    for e in range(EXPERTS):
        line = sum(
            jnp.sum(jnp.where(experts[k] == float(e), at_slot[k], 0.0), axis=0, keepdims=True)
            for k in range(TOP)
        )
        found = sorted_rows[e * pad : (e + 1) * pad]
        packed[e, :, :LANES] = jnp.where(gate_line, line, found[:, :LANES]).astype(bf16)
        packed[e, :, LANES:] = found[:, LANES:].astype(bf16)

    pl.semaphore_wait(barrier, block_count - 1 + len(order) - 1)

    def dispatch(b):
        return pltpu.make_async_remote_copy(
            src_ref=packed.at[b // group_size],
            dst_ref=recv.at[block],
            send_sem=disp_send.at[b],
            recv_sem=disp_recv.at[block],
            device_id=(me, b // tensor_count, b % tensor_count),
            device_id_type=MESH,
        )

    def arrival(b):
        return pltpu.make_async_remote_copy(
            src_ref=packed.at[0],
            dst_ref=recv.at[b],
            send_sem=disp_send.at[0],
            recv_sem=disp_recv.at[b],
            device_id=(me, b // tensor_count, b % tensor_count),
            device_id_type=MESH,
        )

    def remote(src, dst, send, recv_sem, k, device):
        return pltpu.make_async_remote_copy(
            src_ref=src,
            dst_ref=dst,
            send_sem=send.at[k],
            recv_sem=recv_sem.at[k],
            device_id=(device, ctx, tp),
            device_id_type=MESH,
        )

    def to_dp(m):
        return remote(leaving.at[m - 1], landing.at[m], row_send, row_recv, m, order[m])

    def part_to(m):
        return remote(part.at[m], part_in.at[m], part_send, part_recv, m, order[m])

    def to_cross(k):
        return remote(
            saved_in.at[:, piece(k)], saved.at[2, :, piece(k)], cross_send, cross_recv, k, cross
        )

    def to_core(k):
        return remote(
            saved_in.at[:, piece(k)], saved.at[1, :, piece(k)], core_send, core_recv, k, mate
        )

    def pass_on(k):
        return remote(
            saved.at[2, :, piece(k)], saved.at[3, :, piece(k)], pass_send, pass_recv, k, mate
        )

    def send_far(k):
        return remote(
            far_stage.at[:, piece(k)], far_in.at[:, piece(k)], far_send, far_recv, k, mate
        )

    def send_near(k):
        return remote(
            near_stage.at[:, piece(k)], near_in.at[:, piece(k)], near_send, near_recv, k, mate
        )

    @pl.loop(0, block_count)
    def _(b):
        @pl.when(b != block)
        def _():
            dispatch(b).start()

    @pl.loop(0, early)
    def _(k):
        to_cross(k).start()

    recv[block] = packed[block // group_size]
    part[...] = jnp.zeros_like(part)

    @pl.loop(0, block_count)
    def _(b):
        @pl.when(b != block)
        def _():
            arrival(b).wait_recv()

    joined = pick.shape[1] // pad
    spans = [
        (first, pl.ds(first * capacity, joined * capacity))
        for first in range(0, context_count, joined)
    ]

    def block_rows(first, t):
        return jnp.concatenate(
            [recv[(first + c) * tensor_count + t] for c in range(joined)], axis=0
        )

    for first, span in spans:
        gate_lanes = jnp.dot(
            pick_gate[...], block_rows(first, 0)[:, :LANES], preferred_element_type=f32
        )
        gate = jnp.sum(gate_lanes * slot_lane[...], axis=1, keepdims=True)
        gate_out[span, :] = jnp.broadcast_to(gate, (joined * capacity, LANES))
    for m in (3, 2, 1, 0):
        there = leaving.at[m - 1] if m else landing.at[0]
        for first, span in spans:
            value = jnp.dot(pick[...], block_rows(first, order[m]), preferred_element_type=f32)
            there[span, :cols] = value.astype(bf16)
            there[span, cols:] = gate_out[span, :].astype(bf16)
        if m:
            to_dp(m).start()

    @pl.loop(early, chunks)
    def _(k):
        to_cross(k).start()

    @pl.loop(0, chunks)
    def _(k):
        to_core(k).start()

    for m in (1, 2, 3):
        to_dp(m).wait_recv()
    if slots % 16 == 0:
        pieces = [[(m, span)] for m in range(4) for _, span in spans]
    else:
        pieces = [[(m, pl.ds(0, slots)) for m in range(4)]]
    start = 0
    for group in pieces:
        row_values = jnp.concatenate(
            [landing[m, span, :cols].astype(f32) for m, span in group], axis=0
        )
        gate_column = jnp.concatenate(
            [landing[m, span, cols:].astype(f32)[:, :1] for m, span in group], axis=0
        )
        there = pl.ds(start, row_values.shape[0])
        rows[there, :] = row_values.astype(bf16)
        weighted[there, :] = (gate_column * row_values).astype(bf16)
        start += row_values.shape[0]

    @pl.loop(0, chunks)
    def _(k):
        load(k).wait()
        proj = lax.dot_general(
            rows[...],
            weight[piece(k), :],
            (((1,), (1,)), ((), ())),
            preferred_element_type=jnp.float32,
        )
        near_sum[:, piece(k)] = proj[:slots].astype(jnp.bfloat16)
        near_stage[:, piece(k)] = proj[slots : 2 * slots].astype(jnp.bfloat16)
        far_own[:, piece(k)] = proj[2 * slots : 3 * slots].astype(jnp.bfloat16)
        far_stage[:, piece(k)] = proj[3 * slots :].astype(jnp.bfloat16)
        send_far(k).start()
        send_near(k).start()

    own.wait()

    def tally(m, left, right):
        product = left.astype(jnp.float32) * right.astype(jnp.float32)
        total = product[:, :LANES]
        for j in range(1, width // LANES):
            total = total + product[:, j * LANES : (j + 1) * LANES]
        part[m] += total

    @pl.loop(0, chunks)
    def _(k):
        to_cross(k).wait_recv()
        pass_on(k).start()
        to_core(k).wait_recv()
        tally(0, saved[0, :, piece(k)], near_sum[:, piece(k)])
        tally(1, saved[1, :, piece(k)], near_stage[:, piece(k)])
        tally(2, saved[2, :, piece(k)], far_own[:, piece(k)])
        send_far(k).wait_recv()
        far_sum[:, piece(k)] = (
            far_own[:, piece(k)].astype(jnp.float32) + far_in[:, piece(k)].astype(jnp.float32)
        ).astype(jnp.bfloat16)
        send_near(k).wait_recv()
        near_sum[:, piece(k)] = (
            near_sum[:, piece(k)].astype(jnp.float32) + near_in[:, piece(k)].astype(jnp.float32)
        ).astype(jnp.bfloat16)

    @pl.loop(0, chunks)
    def _(k):
        pass_on(k).wait_recv()
        tally(3, saved[3, :, piece(k)], far_stage[:, piece(k)])

    for m in (1, 2, 3):
        part_to(m).start()

    @pl.loop(0, chunks)
    def _(k):
        to_cross(k).wait_send()
        to_core(k).wait_send()
        pass_on(k).wait_send()
        send_far(k).wait_send()
        send_near(k).wait_send()

    @pl.loop(0, block_count)
    def _(b):
        @pl.when(b != block)
        def _():
            dispatch(b).wait_send()

    for m in (1, 2, 3):
        to_dp(m).wait_send()
    for m in (1, 2, 3):
        part_to(m).wait_recv()
    part_sum[...] = (part[0] + part_in[1]) + (part_in[2] + part_in[3])
    for m in (1, 2, 3):
        part_to(m).wait_send()


def run_exchange(
    pad, id_rows, logit_rows, upstream, pick, pick_gate, slot_lane, hidden_saved, down_weight
):
    context_count = lax.axis_size("ctx")
    tensor_count = lax.axis_size("tp")
    block_count = context_count * tensor_count
    slots, hidden = hidden_saved.shape
    cols = down_weight.shape[1]
    chunks = hidden // chunk_width(slots, hidden)
    bf16, f32 = jnp.bfloat16, jnp.float32
    vmem = pl.BlockSpec(memory_space=pltpu.VMEM)
    dma = pltpu.SemaphoreType.DMA
    return pl.pallas_call(
        functools.partial(
            exchange, (context_count, tensor_count, block_count // EXPERTS)
        ),
        out_shape=[
            jax.ShapeDtypeStruct((slots, hidden), bf16),
            jax.ShapeDtypeStruct((slots, hidden), bf16),
            jax.ShapeDtypeStruct((4, slots, hidden), bf16),
            jax.ShapeDtypeStruct((4 * slots, cols), bf16),
            jax.ShapeDtypeStruct((slots, LANES), f32),
            jax.ShapeDtypeStruct((slots, LANES), f32),
        ],
        in_specs=[vmem] * 6 + [pl.BlockSpec(memory_space=pl.ANY)] * 2,
        out_specs=[vmem] * 6,
        scratch_shapes=[
            pltpu.VMEM((EXPERTS, pad, cols), bf16),
            pltpu.VMEM((block_count, pad, cols), bf16),
            pltpu.VMEM((3, slots, cols + LANES), bf16),
            pltpu.VMEM((4, slots, cols + LANES), bf16),
            pltpu.VMEM((hidden, cols), bf16),
            pltpu.VMEM((4 * slots, cols), bf16),
            pltpu.VMEM((slots, hidden), bf16),
            pltpu.VMEM((slots, hidden), bf16),
            pltpu.VMEM((slots, hidden), bf16),
            pltpu.VMEM((slots, hidden), bf16),
            pltpu.VMEM((slots, hidden), bf16),
            pltpu.VMEM((4, slots, LANES), f32),
            pltpu.VMEM((4, slots, LANES), f32),
            dma((block_count,)),
            dma((block_count,)),
            dma((4,)),
            dma((4,)),
            dma((4,)),
            dma((4,)),
        ]
        + [dma((chunks,))] * 11
        + [dma],
        compiler_params=pltpu.CompilerParams(
            collective_id=0, has_side_effects=True, vmem_limit_bytes=60 * 1024 * 1024
        ),
        cost_estimate=pl.CostEstimate(
            flops=8 * slots * hidden * cols, bytes_accessed=2 * hidden * cols, transcendentals=0
        ),
    )(id_rows, logit_rows, upstream, pick, pick_gate, slot_lane, hidden_saved, down_weight)


def local(upstream, router_logits, expert_ids, hidden_saved, down_weight):
    token_count, feature_cols = upstream.shape
    dp_count = lax.axis_size("dp")
    tensor_count = lax.axis_size("tp")
    context_count = lax.axis_size("ctx")
    block_count = context_count * tensor_count
    slots = hidden_saved.shape[0]
    capacity = slots // context_count
    group_size = block_count // EXPERTS
    pad = -(-(capacity + 1) // 16) * 16
    assert dp_count == 4 and tensor_count == dp_count
    assert capacity <= LANES and token_count == LANES

    joined = 4 if context_count % 4 == 0 else context_count
    index = np.arange(joined * capacity)
    first = (index // capacity) * pad
    columns = np.arange(joined * pad)[None, :]
    pick = ((first + index % capacity)[:, None] == columns).astype(jnp.bfloat16)
    pick_gate = ((first + capacity)[:, None] == columns).astype(jnp.bfloat16)
    slot_lane = ((index % capacity)[:, None] == np.arange(LANES)[None, :]).astype(np.float32)

    far_sum, near_sum, saved, weighted, gate_own, part = run_exchange(
        pad,
        expert_ids.T,
        router_logits.T,
        upstream,
        pick,
        pick_gate,
        slot_lane,
        hidden_saved,
        down_weight,
    )
    cross = swap(far_sum, 2)

    part, expert_ids, router_logits = lax.optimization_barrier((part, expert_ids, router_logits))
    part = part.sum(axis=1)
    outgoing = jnp.broadcast_to(
        part.reshape(context_count, 1, capacity), (context_count, tensor_count, capacity)
    ).reshape(block_count, capacity)
    returned = lax.all_to_all(outgoing, ("ctx", "tp"), split_axis=0, concat_axis=0, tiled=True)
    expert_sums = returned.reshape(EXPERTS, group_size, capacity).sum(axis=1)
    gates = 1.0 / (1.0 + jnp.exp(router_logits[:, ::-1] - router_logits))
    onehot = (expert_ids[:, :, None] == jnp.arange(EXPERTS, dtype=jnp.int32)).astype(jnp.float32)
    number = jnp.arange(token_count, dtype=jnp.int32)
    prior = lax.dot_general(
        (number[:, None] > number[None, :]).astype(jnp.bfloat16),
        onehot.sum(axis=1).astype(jnp.bfloat16),
        (((1,), (0,)), ((), ())),
        preferred_element_type=jnp.float32,
    )
    slot = jnp.sum(onehot * prior[:, None, :], axis=2).astype(jnp.int32)
    at_slot = slot[:, :, None] == jnp.arange(capacity, dtype=jnp.int32)
    of_route = jnp.sum(onehot[:, :, :, None] * expert_sums[None, None], axis=2)
    route_grad = jnp.sum(jnp.where(at_slot, of_route, 0.0), axis=2)
    logit_grad = gates * (route_grad - jnp.sum(gates * route_grad, axis=1, keepdims=True))

    down_grad = lax.dot_general(
        saved.reshape(4 * slots, -1),
        weighted,
        (((0,), (0,)), ((), ())),
        preferred_element_type=jnp.float32,
    ).astype(jnp.bfloat16)

    proj = near_sum.astype(jnp.float32) + cross.astype(jnp.float32)
    hidden_grad = (gate_own[:, :1] * proj).astype(jnp.bfloat16)
    return (hidden_grad, down_grad, logit_grad)


def solution(mesh):
    in_specs = (
        P(("dp", "ctx"), "tp"),
        P(("dp", "ctx"), None),
        P(("dp", "ctx"), None),
        P("dp", ("ctx", "tp")),
        P(("ctx", "tp"), "dp"),
    )
    out_specs = (P("dp", ("ctx", "tp")), P(("ctx", "tp"), "dp"), P(("dp", "ctx"), None))
    return jax.shard_map(local, mesh=mesh, in_specs=in_specs, out_specs=out_specs, check_vma=False)
```

time: 90.1 us -> 87.8 us (0.974)
  other arithmetic: 8.27 us -> 3.06 us
  waiting for transfers between devices: 9.82 us -> 13.6 us
  local copies, waits for them, and re-layouts: 3.91 us -> 0.95 us
  Pallas kernels: 46.3 us -> 48.3 us
    ppermute x1, waiting for transfers between devices: 3.61 us -> 13.6 us  [swap(): return lax.ppermute(value, 'dp', [(i, i ^ distance) for i in range(count)])]
    all_to_all x1, waiting for transfers between devices: 6.21 us -> 0.01 us  [local(): lax.all_to_all(outgoing, ('ctx', 'tp'), split_axis=0, concat_axis=0, tile...]
    all_to_all x1, starting transfers between devices: 3.31 us -> 7.79 us  [local(): lax.all_to_all(outgoing, ('ctx', 'tp'), split_axis=0, concat_axis=0, tile...]
    all_to_all x1 -> x0, starting transfers between devices: 3.22 us -> none  [local(): lax.all_to_all(part, 'dp', split_axis=0, concat_axis=0, tiled=True)]
    convert_element_type x5 -> x2, other arithmetic: 2.37 us -> 0.01 us  [the longest x1 0.01 us: local(): (expert_ids[:, :, None] == jnp.arange(EXPERTS, dtype=jnp.int32)).astype(j...]
    unnamed x9 -> x8, local copies, waits for them, and re-layouts: 2.26 us -> 0.02 us
    pallas_call x1, Pallas kernels: 46.3 us -> 48.3 us  [run_exchange(): pl.pallas_call(functools.partial(exchange, (context_count, tensor_count,...]
    convert_element_type x1, other arithmetic: 2.64 us -> 1.38 us  [local(): hidden_grad = (gate_own[:, :1] * proj).astype(jnp.bfloat16)]
  transfers between devices with their start and end apart: 3 -> 2, of which waited for: 2 -> 1; matrix products, arithmetic and copies ran while one was open for 15% -> 15% of each run, Pallas kernels for 0% -> 0%
where the time goes in v3:
time: 87.8 us; the launch traced here: 87.5 us
  Pallas kernels  48.3 us (55%)
  waiting for transfers between devices  13.6 us (15%)
  matrix products  11.6 us (13%)
  starting transfers between devices  9.29 us (11%)
  other arithmetic  3.06 us (3%)
  local copies, waits for them, and re-layouts  0.95 us (1%)
    pallas_call x1, Pallas kernels, run_exchange(): pl.pallas_call(functools.partial(exchange, (context_count, tensor_count,...  48.3 us
    ppermute x1, waiting for transfers between devices, swap(): return lax.ppermute(value, 'dp', [(i, i ^ distance) for i in range(count)])  13.6 us
    dot_general x1, matrix products, local(): lax.dot_general(saved.reshape(4 * slots, -1), weighted, (((0,), (0,)), ((...  11.5 us
    all_to_all x1, starting transfers between devices, local(): lax.all_to_all(outgoing, ('ctx', 'tp'), split_axis=0, concat_axis=0, tile...  7.79 us
  transfers between devices with their start and end apart: 2, of which 1 were waited for; matrix products, arithmetic and copies ran while one was open for 15% of the time, Pallas kernels for 0%

profile of v3, /device:TPU:0, one launch (start us, length us, event | category | flops | bytes accessed | tf_op | source)
XLA Modules:
  0.0 87.5 jit_solution(18115869392940981873)
XLA Ops:
  0.6 0.0 copy-start.2
  0.6 48.3 %shard_map.103 = (bf16[72,8192]{1,0:T(8,128)(2,1)}, bf16[72,8192]{1,0:T(8,128)(2,1)}, bf16[4,72,8192]{2,1,0:T(8,128)(2,1)}, bf16[288,768]{1,0:T(8,128)(2,1)}, f32[72,128]{1,0:T(8,128)}, /*index=5*/f32[72,128]{1,0:T(8,128)}) custom-call(s32[2,128]{1,0:T(2,128)} %bitcast.9, f32[2,128]{1,0:T(2,128)} %bitcast.10, bf16[128,768]{1,0:T(8,128)(2,1)} %upstream.1, ...), custom_call_target="tpu_custom_call" | custom-call | flops 3623878656 | bytes 12582912 | tf_op jit(solution)/shard_map/pallas_call | solution.py:383
  48.9 0.9 reduce_sum.60
  49.8 0.1 broadcast_in_dim.7
  49.9 0.6 broadcast_in_dim.8
  50.5 7.8 %all-to-all-start = ((f32[8,1,36]{2,1,0:T(1,128)}), f32[8,1,36]{2,1,0:T(1,128)S(1)}, u32[]{:S(2)}, u32[]{:S(2)}) async-start(f32[8,1,36]{2,1,0:T(1,128)} %bitcast.3), calls=%async_computation | async-start | bytes 8192 | tf_op jit(solution)/shard_map/all_to_all | solution.py:468
  58.3 1.5 %collective-permute-start = (bf16[72,8192]{1,0:T(8,128)(2,1)}, bf16[72,8192]{1,0:T(8,128)(2,1)S(1)}, u32[]{:S(2)}, u32[]{:S(2)}) collective-permute-start(bf16[72,8192]{1,0:T(8,128)(2,1)} %get-tuple-element.14), channel_id=1, source_target_pairs={{0,16},{8,24},{16,0},{24,8},{1,17},{9,25},{17,1},{25,9},{2,18},{10... | collective-permute-start | bytes 3538952 | tf_op jit(solution)/shard_map/ppermute | solution.py:19
  59.8 0.0 copy-done.2
  59.8 0.0 copy-start.1
  59.8 0.0 copy-start.3
  59.8 0.0 copy-start
  59.8 11.5 %convolution_convert_fusion = bf16[8192,768]{1,0:T(8,128)(2,1)} fusion(bf16[288,8192]{1,0:T(8,128)(2,1)} %bitcast.11, bf16[288,768]{1,0:T(8,128)(2,1)} %get-tuple-element.16), kind=kOutput, calls=%fused_computation | convolution fusion | flops 3630170112 | bytes 17743872 | tf_op jit(solution)/shard_map/dot_general | solution.py:485
  71.3 0.1 fusion
  71.5 0.0 copy-done.1
  71.5 0.1 slice_reduce_fusion
  71.6 0.0 copy-done.3
  71.7 0.0 all-to-all-done
  71.7 0.1 copy.17
  71.8 0.1 multiply_reduce_fusion
  72.0 0.6 subtract_multiply_fusion
  72.5 13.6 %collective-permute-done = bf16[72,8192]{1,0:T(8,128)(2,1)S(1)} collective-permute-done((bf16[72,8192]{1,0:T(8,128)(2,1)}, bf16[72,8192]{1,0:T(8,128)(2,1)S(1)}, u32[]{:S(2)}, u32[]{:S(2)}) %collective-permute-start) | collective-permute-done | bytes 1179680 | tf_op jit(solution)/shard_map/ppermute | solution.py:19
  86.1 0.0 copy-done
  86.1 1.4 %multiply_convert_fusion = bf16[72,8192]{1,0:T(8,128)(2,1)} fusion(bf16[72,8192]{1,0:T(8,128)(2,1)S(1)} %collective-permute-done, bf16[72,8192]{1,0:T(8,128)(2,1)S(1)} %copy-done, f32[72]{0:T(128)S(1)} %slice_reduce_fusion), kind=kLoop, calls=%fused_computation.1 | loop fusion | flops 2949120 | bytes 3539232 | tf_op jit(solution)/shard_map/convert_element_type | solution.py:493
  (7 shorter events, 0.1 us)
Async XLA Ops:
  0.6 59.2 %copy-start.2 = (s32[128,2]{0,1:T(2,128)S(1)}, s32[128,2]{0,1:T(2,128)}, u32[]{:S(2)}) copy-start(s32[128,2]{0,1:T(2,128)} %param.10) | copy-start | bytes 3076
  50.5 21.2 %all-to-all-start = ((f32[8,1,36]{2,1,0:T(1,128)}), f32[8,1,36]{2,1,0:T(1,128)S(1)}, u32[]{:S(2)}, u32[]{:S(2)}) async-start(f32[8,1,36]{2,1,0:T(1,128)} %bitcast.3), calls=%async_computation | async-start | bytes 8192 | tf_op jit(solution)/shard_map/all_to_all | solution.py:468
  58.3 27.8 %collective-permute-start = (bf16[72,8192]{1,0:T(8,128)(2,1)}, bf16[72,8192]{1,0:T(8,128)(2,1)S(1)}, u32[]{:S(2)}, u32[]{:S(2)}) collective-permute-start(bf16[72,8192]{1,0:T(8,128)(2,1)} %get-tuple-element.14), channel_id=1, source_target_pairs={{0,16},{8,24},{16,0},{24,8},{1,17},{9,25},{17,1},{25,9},{2,18},{10... | collective-permute-start | bytes 3538952 | tf_op jit(solution)/shard_map/ppermute | solution.py:19
  59.8 11.7 %copy-start.1 = (f32[72,128]{1,0:T(8,128)S(1)}, f32[72,128]{1,0:T(8,128)}, u32[]{:S(2)}) copy-start(f32[72,128]{1,0:T(8,128)} %get-tuple-element.12) | copy-start | bytes 110596
  59.8 11.8 %copy-start.3 = (f32[128,2]{0,1:T(2,128)S(1)}, f32[128,2]{0,1:T(2,128)}, u32[]{:S(2)}) copy-start(f32[128,2]{0,1:T(2,128)} %param.9) | copy-start | bytes 3076
  59.8 26.3 %copy-start = (bf16[72,8192]{1,0:T(8,128)(2,1)S(1)}, bf16[72,8192]{1,0:T(8,128)(2,1)}, u32[]{:S(2)}) copy-start(bf16[72,8192]{1,0:T(8,128)(2,1)} %get-tuple-element.13) | copy-start | bytes 3538948

commit v4 on v3

--- a/solution.py
+++ b/solution.py
@@ -21,6 +21,10 @@
 
 def chunk_width(slots, hidden):
     return min(1024 if slots <= 256 else 128, hidden)
+
+
+def head_chunks(chunks):
+    return chunks // 4
 
 
 def exchange(
@@ -52,12 +56,16 @@
     near_in,
     part,
     part_in,
+    far_head,
+    cross_head,
     disp_send,
     disp_recv,
     row_send,
     row_recv,
     part_send,
     part_recv,
+    head_send,
+    head_recv,
     cross_send,
     cross_recv,
     core_send,
@@ -79,7 +87,9 @@
     hidden = saved.shape[2]
     width = chunk_width(slots, hidden)
     chunks = hidden // width
-    early = min(3, chunks)
+    early = chunks * 5 // 8
+    head = head_chunks(chunks)
+    head_width = head * width
     pad = packed.shape[1]
     me = lax.axis_index("dp")
     ctx = lax.axis_index("ctx")
@@ -223,11 +233,9 @@
             near_stage.at[:, piece(k)], near_in.at[:, piece(k)], near_send, near_recv, k, mate
         )
 
-    @pl.loop(0, block_count)
-    def _(b):
-        @pl.when(b != block)
-        def _():
-            dispatch(b).start()
+    @pl.loop(1, block_count)
+    def _(j):
+        dispatch((block + j) % block_count).start()
 
     @pl.loop(0, early)
     def _(k):
@@ -311,6 +319,22 @@
         send_far(k).start()
         send_near(k).start()
 
+    def far_total(k):
+        return (
+            far_own[:, piece(k)].astype(jnp.float32) + far_in[:, piece(k)].astype(jnp.float32)
+        ).astype(jnp.bfloat16)
+
+    def to_head(k):
+        return remote(
+            far_head.at[:, piece(k)], cross_head.at[:, piece(k)], head_send, head_recv, k, cross
+        )
+
+    @pl.loop(0, head)
+    def _(k):
+        send_far(k).wait_recv()
+        far_head[:, piece(k)] = far_total(k)
+        to_head(k).start()
+
     own.wait()
 
     def tally(m, left, right):
@@ -328,10 +352,11 @@
         tally(0, saved[0, :, piece(k)], near_sum[:, piece(k)])
         tally(1, saved[1, :, piece(k)], near_stage[:, piece(k)])
         tally(2, saved[2, :, piece(k)], far_own[:, piece(k)])
-        send_far(k).wait_recv()
-        far_sum[:, piece(k)] = (
-            far_own[:, piece(k)].astype(jnp.float32) + far_in[:, piece(k)].astype(jnp.float32)
-        ).astype(jnp.bfloat16)
+        @pl.when(k >= head)
+        def _():
+            send_far(k).wait_recv()
+            far_sum[:, piece(k - head)] = far_total(k)
+
         send_near(k).wait_recv()
         near_sum[:, piece(k)] = (
             near_sum[:, piece(k)].astype(jnp.float32) + near_in[:, piece(k)].astype(jnp.float32)
@@ -344,6 +369,13 @@
 
     for m in (1, 2, 3):
         part_to(m).start()
+
+    @pl.loop(0, head)
+    def _(k):
+        to_head(k).wait_recv()
+        near_sum[:, piece(k)] = (
+            near_sum[:, piece(k)].astype(jnp.float32) + cross_head[:, piece(k)].astype(jnp.float32)
+        ).astype(jnp.bfloat16)
 
     @pl.loop(0, chunks)
     def _(k):
@@ -358,6 +390,10 @@
         @pl.when(b != block)
         def _():
             dispatch(b).wait_send()
+
+    @pl.loop(0, head)
+    def _(k):
+        to_head(k).wait_send()
 
     for m in (1, 2, 3):
         to_dp(m).wait_send()
@@ -377,6 +413,7 @@
     slots, hidden = hidden_saved.shape
     cols = down_weight.shape[1]
     chunks = hidden // chunk_width(slots, hidden)
+    head_width = head_chunks(chunks) * (hidden // chunks)
     bf16, f32 = jnp.bfloat16, jnp.float32
     vmem = pl.BlockSpec(memory_space=pltpu.VMEM)
     dma = pltpu.SemaphoreType.DMA
@@ -385,7 +422,7 @@
             exchange, (context_count, tensor_count, block_count // EXPERTS)
         ),
         out_shape=[
-            jax.ShapeDtypeStruct((slots, hidden), bf16),
+            jax.ShapeDtypeStruct((slots, hidden - head_width), bf16),
             jax.ShapeDtypeStruct((slots, hidden), bf16),
             jax.ShapeDtypeStruct((4, slots, hidden), bf16),
             jax.ShapeDtypeStruct((4 * slots, cols), bf16),
@@ -408,12 +445,16 @@
             pltpu.VMEM((slots, hidden), bf16),
             pltpu.VMEM((4, slots, LANES), f32),
             pltpu.VMEM((4, slots, LANES), f32),
+            pltpu.VMEM((slots, head_width), bf16),
+            pltpu.VMEM((slots, head_width), bf16),
             dma((block_count,)),
             dma((block_count,)),
             dma((4,)),
             dma((4,)),
             dma((4,)),
             dma((4,)),
+            dma((head_chunks(chunks),)),
+            dma((head_chunks(chunks),)),
         ]
         + [dma((chunks,))] * 11
         + [dma],
@@ -460,7 +501,16 @@
     )
     cross = swap(far_sum, 2)
 
-    part, expert_ids, router_logits = lax.optimization_barrier((part, expert_ids, router_logits))
+    down_grad = lax.dot_general(
+        saved.reshape(4 * slots, -1),
+        weighted,
+        (((0,), (0,)), ((), ())),
+        preferred_element_type=jnp.float32,
+    ).astype(jnp.bfloat16)
+
+    part, expert_ids, router_logits, down_grad = lax.optimization_barrier(
+        (part, expert_ids, router_logits, down_grad)
+    )
     part = part.sum(axis=1)
     outgoing = jnp.broadcast_to(
         part.reshape(context_count, 1, capacity), (context_count, tensor_count, capacity)
@@ -482,13 +532,7 @@
     route_grad = jnp.sum(jnp.where(at_slot, of_route, 0.0), axis=2)
     logit_grad = gates * (route_grad - jnp.sum(gates * route_grad, axis=1, keepdims=True))
 
-    down_grad = lax.dot_general(
-        saved.reshape(4 * slots, -1),
-        weighted,
-        (((0,), (0,)), ((), ())),
-        preferred_element_type=jnp.float32,
-    ).astype(jnp.bfloat16)
-
+    cross = jnp.pad(cross, ((0, 0), (near_sum.shape[1] - cross.shape[1], 0)))
     proj = near_sum.astype(jnp.float32) + cross.astype(jnp.float32)
     hidden_grad = (gate_own[:, :1] * proj).astype(jnp.bfloat16)
     return (hidden_grad, down_grad, logit_grad)

time: 87.8 us -> 77.2 us (0.88)
  waiting for transfers between devices: 13.6 us -> 6.04 us
  starting transfers between devices: 9.29 us -> 3.97 us
  Pallas kernels: 48.3 us -> 51.5 us
    ppermute x1, waiting for transfers between devices: 13.6 us -> 0.01 us  [swap(): return lax.ppermute(value, 'dp', [(i, i ^ distance) for i in range(count)])]
    all_to_all x1, waiting for transfers between devices: 0.01 us -> 6.03 us  [local(): lax.all_to_all(outgoing, ('ctx', 'tp'), split_axis=0, concat_axis=0, tile...]
    all_to_all x1, starting transfers between devices: 7.79 us -> 3.37 us  [local(): lax.all_to_all(outgoing, ('ctx', 'tp'), split_axis=0, concat_axis=0, tile...]
    pallas_call x1, Pallas kernels: 48.3 us -> 51.5 us  [run_exchange(): pl.pallas_call(functools.partial(exchange, (context_count, tensor_count,...]
    ppermute x1, starting transfers between devices: 1.49 us -> 0.6 us  [swap(): return lax.ppermute(value, 'dp', [(i, i ^ distance) for i in range(count)])]
  transfers between devices with their start and end apart: 2 -> 2, of which waited for: 1 -> 1; matrix products, arithmetic and copies ran while one was open for 15% -> 18% of each run, Pallas kernels for 0% -> 0%
where the time goes in v4:
time: 77.2 us; the launch traced here: 77 us
  Pallas kernels  51.5 us (67%)
  matrix products  11.6 us (15%)
  waiting for transfers between devices  6.04 us (8%)
  starting transfers between devices  3.97 us (5%)
  other arithmetic  2.27 us (3%)
  local copies, waits for them, and re-layouts  0.95 us (1%)
    pallas_call x1, Pallas kernels, run_exchange(): pl.pallas_call(functools.partial(exchange, (context_count, tensor_count,...  51.5 us
    dot_general x1, matrix products, local(): lax.dot_general(saved.reshape(4 * slots, -1), weighted, (((0,), (0,)), ((...  11.5 us
    all_to_all x1, waiting for transfers between devices, local(): lax.all_to_all(outgoing, ('ctx', 'tp'), split_axis=0, concat_axis=0, tile...  6.03 us
    all_to_all x1, starting transfers between devices, local(): lax.all_to_all(outgoing, ('ctx', 'tp'), split_axis=0, concat_axis=0, tile...  3.37 us
  transfers between devices with their start and end apart: 2, of which 1 were waited for; matrix products, arithmetic and copies ran while one was open for 18% of the time, Pallas kernels for 0%

profile of v4, /device:TPU:0, one launch (start us, length us, event | category | flops | bytes accessed | tf_op | source)
XLA Modules:
  0.0 77.0 jit_solution(7118250038228833620)
XLA Ops:
  0.6 51.5 %shard_map.103 = (bf16[72,6144]{1,0:T(8,128)(2,1)}, bf16[72,8192]{1,0:T(8,128)(2,1)}, bf16[4,72,8192]{2,1,0:T(8,128)(2,1)}, bf16[288,768]{1,0:T(8,128)(2,1)}, f32[72,128]{1,0:T(8,128)}, /*index=5*/f32[72,128]{1,0:T(8,128)}) custom-call(s32[2,128]{1,0:T(2,128)} %bitcast.9, f32[2,128]{1,0:T(2,128)} %bitcast.10, bf16[128,768]{1,0:T(8,128)(2,1)} %upstream.1, ...), custom_call_target="tpu_custom_call" | custom-call | flops 3623878656 | bytes 12582912 | tf_op jit(solution)/shard_map/pallas_call | solution.py:420
  52.1 0.6 collective-permute-start
  52.7 0.0 copy-start.2
  52.7 0.0 copy-start.3
  52.7 0.0 copy-start.1
  52.7 0.0 copy-start.4
  52.7 0.0 copy-start
  52.7 11.5 %convolution_convert_fusion = bf16[8192,768]{1,0:T(8,128)(2,1)} fusion(bf16[288,8192]{1,0:T(8,128)(2,1)} %bitcast.11, bf16[288,768]{1,0:T(8,128)(2,1)} %get-tuple-element.18), kind=kOutput, calls=%fused_computation | convolution fusion | flops 3630170112 | bytes 17743872 | tf_op jit(solution)/shard_map/dot_general | solution.py:504
  64.2 0.0 copy-done.2
  64.2 0.1 reduce_sum.60
  64.3 0.1 broadcast_in_dim.7
  64.4 0.6 broadcast_in_dim.8
  65.0 3.4 %all-to-all-start = ((f32[8,1,36]{2,1,0:T(1,128)}), f32[8,1,36]{2,1,0:T(1,128)S(1)}, u32[]{:S(2)}, u32[]{:S(2)}) async-start(f32[8,1,36]{2,1,0:T(1,128)} %bitcast.3), calls=%async_computation | async-start | bytes 8192 | tf_op jit(solution)/shard_map/all_to_all | solution.py:518
  68.4 0.0 copy-done.3
  68.4 0.1 fusion
  68.6 0.0 copy-done.1
  68.6 0.1 slice_reduce_fusion
  68.7 0.0 copy-done.4
  68.8 6.0 %all-to-all-done = f32[8,1,36]{2,1,0:T(1,128)S(1)} async-done(((f32[8,1,36]{2,1,0:T(1,128)}), f32[8,1,36]{2,1,0:T(1,128)S(1)}, u32[]{:S(2)}, u32[]{:S(2)}) %all-to-all-start) | async-done | bytes 1184 | tf_op jit(solution)/shard_map/all_to_all | solution.py:518
  74.8 0.1 copy.17
  74.9 0.1 multiply_reduce_fusion
  75.1 0.6 subtract_multiply_fusion
  75.7 0.0 collective-permute-done
  75.7 0.0 copy-done
  75.7 1.4 %multiply_convert_fusion = bf16[72,8192]{1,0:T(8,128)(2,1)} fusion(bf16[72,8192]{1,0:T(8,128)(2,1)S(1)} %copy-done, bf16[72,6144]{1,0:T(8,128)(2,1)S(1)} %collective-permute-done, f32[72]{0:T(128)S(1)} %slice_reduce_fusion), kind=kLoop, calls=%fused_computation.1 | loop fusion | flops 2949120 | bytes 3244320 | tf_op jit(solution)/shard_map/convert_element_type | solution.py:537
  (7 shorter events, 0.1 us)
Async XLA Ops:
  52.1 23.6 %collective-permute-start = (bf16[72,6144]{1,0:T(8,128)(2,1)}, bf16[72,6144]{1,0:T(8,128)(2,1)S(1)}, u32[]{:S(2)}, u32[]{:S(2)}) collective-permute-start(bf16[72,6144]{1,0:T(8,128)(2,1)} %get-tuple-element.15), channel_id=1, source_target_pairs={{0,16},{8,24},{16,0},{24,8},{1,17},{9,25},{17,1},{25,9},{2,18},{10... | collective-permute-start | bytes 2654216 | tf_op jit(solution)/shard_map/ppermute | solution.py:19
  52.7 11.5 %copy-start.2 = (f32[72,128]{1,0:T(8,128)S(1)}, f32[72,128]{1,0:T(8,128)}, u32[]{:S(2)}) copy-start(f32[72,128]{1,0:T(8,128)} %get-tuple-element.22) | copy-start | bytes 110596
  52.7 15.7 %copy-start.3 = (s32[128,2]{0,1:T(2,128)S(1)}, s32[128,2]{0,1:T(2,128)}, u32[]{:S(2)}) copy-start(s32[128,2]{0,1:T(2,128)} %param.10) | copy-start | bytes 3076
  52.7 15.9 %copy-start.1 = (f32[72,128]{1,0:T(8,128)S(1)}, f32[72,128]{1,0:T(8,128)}, u32[]{:S(2)}) copy-start(f32[72,128]{1,0:T(8,128)} %get-tuple-element.13) | copy-start | bytes 110596
  52.7 16.0 %copy-start.4 = (f32[128,2]{0,1:T(2,128)S(1)}, f32[128,2]{0,1:T(2,128)}, u32[]{:S(2)}) copy-start(f32[128,2]{0,1:T(2,128)} %param.9) | copy-start | bytes 3076
  52.7 23.0 %copy-start = (bf16[72,8192]{1,0:T(8,128)(2,1)S(1)}, bf16[72,8192]{1,0:T(8,128)(2,1)}, u32[]{:S(2)}) copy-start(bf16[72,8192]{1,0:T(8,128)(2,1)} %get-tuple-element.14) | copy-start | bytes 3538948
  65.0 9.8 %all-to-all-start = ((f32[8,1,36]{2,1,0:T(1,128)}), f32[8,1,36]{2,1,0:T(1,128)S(1)}, u32[]{:S(2)}, u32[]{:S(2)}) async-start(f32[8,1,36]{2,1,0:T(1,128)} %bitcast.3), calls=%async_computation | async-start | bytes 8192 | tf_op jit(solution)/shard_map/all_to_all | solution.py:518

commit v5 on v4

--- a/solution.py
+++ b/solution.py
@@ -39,7 +39,7 @@
     weight_in,
     far_sum,
     near_sum,
-    saved,
+    saved_out,
     weighted,
     gate_out,
     part_sum,
@@ -56,6 +56,7 @@
     near_in,
     part,
     part_in,
+    saved,
     far_head,
     cross_head,
     disp_send,
@@ -77,6 +78,7 @@
     near_send,
     near_recv,
     weight_sem,
+    out_sem,
     own_sem,
 ):
     context_count, tensor_count, group_size = sizes
@@ -107,6 +109,11 @@
             weight_in.at[piece(k), :], weight.at[piece(k), :], weight_sem.at[k]
         )
 
+    def write_out(k):
+        return pltpu.make_async_copy(
+            saved.at[:, :, piece(k)], saved_out.at[:, :, piece(k)], out_sem.at[k]
+        )
+
     own = pltpu.make_async_copy(saved_in, saved.at[0], own_sem)
 
     barrier = pltpu.get_barrier_semaphore()
@@ -365,6 +372,7 @@
     @pl.loop(0, chunks)
     def _(k):
         pass_on(k).wait_recv()
+        write_out(k).start()
         tally(3, saved[3, :, piece(k)], far_stage[:, piece(k)])
 
     for m in (1, 2, 3):
@@ -379,6 +387,7 @@
 
     @pl.loop(0, chunks)
     def _(k):
+        write_out(k).wait()
         to_cross(k).wait_send()
         to_core(k).wait_send()
         pass_on(k).wait_send()
@@ -430,7 +439,7 @@
             jax.ShapeDtypeStruct((slots, LANES), f32),
         ],
         in_specs=[vmem] * 6 + [pl.BlockSpec(memory_space=pl.ANY)] * 2,
-        out_specs=[vmem] * 6,
+        out_specs=[vmem] * 2 + [pl.BlockSpec(memory_space=pl.ANY)] + [vmem] * 3,
         scratch_shapes=[
             pltpu.VMEM((EXPERTS, pad, cols), bf16),
             pltpu.VMEM((block_count, pad, cols), bf16),
@@ -445,6 +454,7 @@
             pltpu.VMEM((slots, hidden), bf16),
             pltpu.VMEM((4, slots, LANES), f32),
             pltpu.VMEM((4, slots, LANES), f32),
+            pltpu.VMEM((4, slots, hidden), bf16),
             pltpu.VMEM((slots, head_width), bf16),
             pltpu.VMEM((slots, head_width), bf16),
             dma((block_count,)),
@@ -456,7 +466,7 @@
             dma((head_chunks(chunks),)),
             dma((head_chunks(chunks),)),
         ]
-        + [dma((chunks,))] * 11
+        + [dma((chunks,))] * 12
         + [dma],
         compiler_params=pltpu.CompilerParams(
             collective_id=0, has_side_effects=True, vmem_limit_bytes=60 * 1024 * 1024
@@ -465,6 +475,34 @@
             flops=8 * slots * hidden * cols, bytes_accessed=2 * hidden * cols, transcendentals=0
         ),
     )(id_rows, logit_rows, upstream, pick, pick_gate, slot_lane, hidden_saved, down_weight)
+
+
+def gradient_block(saved, weighted, out):
+    out[...] = lax.dot_general(
+        saved[...], weighted[...], (((0,), (0,)), ((), ())), preferred_element_type=jnp.float32
+    ).astype(jnp.bfloat16)
+
+
+def weight_gradient(saved, weighted):
+    depth, hidden = saved.shape
+    cols = weighted.shape[1]
+    block = min(1024 if depth <= 1024 else 256, hidden)
+    return pl.pallas_call(
+        gradient_block,
+        grid=(hidden // block,),
+        out_shape=jax.ShapeDtypeStruct((hidden, cols), jnp.bfloat16),
+        in_specs=[
+            pl.BlockSpec((depth, block), lambda i: (0, i)),
+            pl.BlockSpec((depth, cols), lambda i: (0, 0)),
+        ],
+        out_specs=pl.BlockSpec((block, cols), lambda i: (i, 0)),
+        compiler_params=pltpu.CompilerParams(vmem_limit_bytes=60 * 1024 * 1024),
+        cost_estimate=pl.CostEstimate(
+            flops=2 * depth * hidden * cols,
+            bytes_accessed=2 * (depth * hidden + depth * cols + hidden * cols),
+            transcendentals=0,
+        ),
+    )(saved, weighted)
 
 
 def local(upstream, router_logits, expert_ids, hidden_saved, down_weight):
@@ -501,12 +539,7 @@
     )
     cross = swap(far_sum, 2)
 
-    down_grad = lax.dot_general(
-        saved.reshape(4 * slots, -1),
-        weighted,
-        (((0,), (0,)), ((), ())),
-        preferred_element_type=jnp.float32,
-    ).astype(jnp.bfloat16)
+    down_grad = weight_gradient(saved.reshape(4 * slots, -1), weighted)
 
     part, expert_ids, router_logits, down_grad = lax.optimization_barrier(
         (part, expert_ids, router_logits, down_grad)

time: 77.2 us -> 76.9 us (level)
  matrix products: 11.6 us -> 0.13 us
  Pallas kernels: 51.5 us -> 62.5 us
    pallas_call x0 -> x1, Pallas kernels: none -> 12.3 us  [weight_gradient(): pl.pallas_call(gradient_block, grid=(hidden // block,), out_shape=jax.Sha...]
    dot_general x1 -> x0, matrix products: 11.5 us -> none  [local(): lax.dot_general(saved.reshape(4 * slots, -1), weighted, (((0,), (0,)), ((...]
    pallas_call x1, Pallas kernels: 51.5 us -> 50.1 us  [run_exchange(): pl.pallas_call(functools.partial(exchange, (context_count, tensor_count,...]
  transfers between devices with their start and end apart: 2 -> 2, of which waited for: 1 -> 1; matrix products, arithmetic and copies ran while one was open for 18% -> 3% of each run, Pallas kernels for 0% -> 16%
where the time goes in v5:
time: 76.9 us; the launch traced here: 76.5 us
  Pallas kernels  62.5 us (81%)
  waiting for transfers between devices  6.04 us (8%)
  starting transfers between devices  3.96 us (5%)
  other arithmetic  2.27 us (3%)
  local copies, waits for them, and re-layouts  0.95 us (1%)
    pallas_call x1, Pallas kernels, run_exchange(): pl.pallas_call(functools.partial(exchange, (context_count, tensor_count,...  50.1 us
    pallas_call x1, Pallas kernels, weight_gradient(): pl.pallas_call(gradient_block, grid=(hidden // block,), out_shape=jax.Sha...  12.3 us
    all_to_all x1, waiting for transfers between devices, local(): lax.all_to_all(outgoing, ('ctx', 'tp'), split_axis=0, concat_axis=0, tile...  6.03 us
    all_to_all x1, starting transfers between devices, local(): lax.all_to_all(outgoing, ('ctx', 'tp'), split_axis=0, concat_axis=0, tile...  3.36 us
  transfers between devices with their start and end apart: 2, of which 1 were waited for; matrix products, arithmetic and copies ran while one was open for 3% of the time, Pallas kernels for 16%

profile of v5, /device:TPU:0, one launch (start us, length us, event | category | flops | bytes accessed | tf_op | source)
XLA Modules:
  0.0 76.5 jit_solution(18377841845450491709)
XLA Ops:
  0.6 50.1 %shard_map.103 = (bf16[72,6144]{1,0:T(8,128)(2,1)}, bf16[72,8192]{1,0:T(8,128)(2,1)}, bf16[4,72,8192]{2,1,0:T(8,128)(2,1)}, bf16[288,768]{1,0:T(8,128)(2,1)}, f32[72,128]{1,0:T(8,128)}, /*index=5*/f32[72,128]{1,0:T(8,128)}) custom-call(s32[2,128]{1,0:T(2,128)} %bitcast.8, f32[2,128]{1,0:T(2,128)} %bitcast.9, bf16[128,768]{1,0:T(8,128)(2,1)} %upstream.1, ...), custom_call_target="tpu_custom_call" | custom-call | flops 3623878656 | bytes 12582912 | tf_op jit(solution)/shard_map/pallas_call | solution.py:429
  50.8 0.6 collective-permute-start
  51.4 0.0 copy-start.2
  51.4 0.0 copy-start.3
  51.4 0.0 copy-start.1
  51.4 0.0 copy-start.4
  51.4 0.0 copy-start
  51.4 12.3 %shard_map.104 = bf16[8192,768]{1,0:T(8,128)(2,1)} custom-call(bf16[288,8192]{1,0:T(8,128)(2,1)} %bitcast.6, bf16[288,768]{1,0:T(8,128)(2,1)} %get-tuple-element.18.weighted), custom_call_target="tpu_custom_call" | custom-call | flops 3623878656 | bytes 17743872 | tf_op jit(solution)/shard_map/pallas_call | solution.py:490
  63.7 0.0 copy-done.2
  63.7 0.1 reduce_sum.60
  63.8 0.1 broadcast_in_dim.7
  63.9 0.6 broadcast_in_dim.8
  64.5 3.4 %all-to-all-start = ((f32[8,1,36]{2,1,0:T(1,128)}), f32[8,1,36]{2,1,0:T(1,128)S(1)}, u32[]{:S(2)}, u32[]{:S(2)}) async-start(f32[8,1,36]{2,1,0:T(1,128)} %bitcast.3), calls=%async_computation | async-start | bytes 8192 | tf_op jit(solution)/shard_map/all_to_all | solution.py:551
  67.9 0.0 copy-done.3
  67.9 0.1 fusion
  68.1 0.0 copy-done.1
  68.1 0.1 slice_reduce_fusion
  68.2 0.0 copy-done.4
  68.2 6.0 %all-to-all-done = f32[8,1,36]{2,1,0:T(1,128)S(1)} async-done(((f32[8,1,36]{2,1,0:T(1,128)}), f32[8,1,36]{2,1,0:T(1,128)S(1)}, u32[]{:S(2)}, u32[]{:S(2)}) %all-to-all-start) | async-done | bytes 1184 | tf_op jit(solution)/shard_map/all_to_all | solution.py:551
  74.3 0.1 copy.17
  74.4 0.1 multiply_reduce_fusion
  74.6 0.6 subtract_multiply_fusion
  75.2 0.0 collective-permute-done
  75.2 0.0 copy-done
  75.2 1.4 %multiply_convert_fusion = bf16[72,8192]{1,0:T(8,128)(2,1)} fusion(bf16[72,8192]{1,0:T(8,128)(2,1)S(1)} %copy-done, bf16[72,6144]{1,0:T(8,128)(2,1)S(1)} %collective-permute-done, f32[72]{0:T(128)S(1)} %slice_reduce_fusion), kind=kLoop, calls=%fused_computation | loop fusion | flops 2949120 | bytes 3244320 | tf_op jit(solution)/shard_map/convert_element_type | solution.py:570
  (7 shorter events, 0.1 us)
Async XLA Ops:
  50.8 24.4 %collective-permute-start = (bf16[72,6144]{1,0:T(8,128)(2,1)}, bf16[72,6144]{1,0:T(8,128)(2,1)S(1)}, u32[]{:S(2)}, u32[]{:S(2)}) collective-permute-start(bf16[72,6144]{1,0:T(8,128)(2,1)} %get-tuple-element.15), channel_id=1, source_target_pairs={{0,16},{8,24},{16,0},{24,8},{1,17},{9,25},{17,1},{25,9},{2,18},{10... | collective-permute-start | bytes 2654216 | tf_op jit(solution)/shard_map/ppermute | solution.py:19
  51.4 12.4 %copy-start.2 = (f32[72,128]{1,0:T(8,128)S(1)}, f32[72,128]{1,0:T(8,128)}, u32[]{:S(2)}) copy-start(f32[72,128]{1,0:T(8,128)} %get-tuple-element.22) | copy-start | bytes 110596
  51.4 16.5 %copy-start.3 = (s32[128,2]{0,1:T(2,128)S(1)}, s32[128,2]{0,1:T(2,128)}, u32[]{:S(2)}) copy-start(s32[128,2]{0,1:T(2,128)} %param.10) | copy-start | bytes 3076
  51.4 16.7 %copy-start.1 = (f32[72,128]{1,0:T(8,128)S(1)}, f32[72,128]{1,0:T(8,128)}, u32[]{:S(2)}) copy-start(f32[72,128]{1,0:T(8,128)} %get-tuple-element.13) | copy-start | bytes 110596
  51.4 16.8 %copy-start.4 = (f32[128,2]{0,1:T(2,128)S(1)}, f32[128,2]{0,1:T(2,128)}, u32[]{:S(2)}) copy-start(f32[128,2]{0,1:T(2,128)} %param.9) | copy-start | bytes 3076
  51.4 23.8 %copy-start = (bf16[72,8192]{1,0:T(8,128)(2,1)S(1)}, bf16[72,8192]{1,0:T(8,128)(2,1)}, u32[]{:S(2)}) copy-start(bf16[72,8192]{1,0:T(8,128)(2,1)} %get-tuple-element.14) | copy-start | bytes 3538948
  64.5 9.8 %all-to-all-start = ((f32[8,1,36]{2,1,0:T(1,128)}), f32[8,1,36]{2,1,0:T(1,128)S(1)}, u32[]{:S(2)}, u32[]{:S(2)}) async-start(f32[8,1,36]{2,1,0:T(1,128)} %bitcast.3), calls=%async_computation | async-start | bytes 8192 | tf_op jit(solution)/shard_map/all_to_all | solution.py:551
